TPU v7x, 128 devices: a whole 4x4x4 slice. The times are simulated.
128 devices in a mesh: section: 4 (over x), blk: 4 (over z_lo, core), uly: 8 (over z_hi, y).
Axes of the slice: x: 4, y: 4, z: 4 (z_hi: 2, z_lo: 2; z = z_hi * 2 + z_lo), core: 2. Of those that a mesh axis runs over, the one named last changes fastest.
Arguments:
- queries: bfloat16 [4, 4096, 5120], P('section', ('blk', 'uly')), may hold values from -4.5 to 4.5
- keys: bfloat16 [4, 4096, 1024], P('section', ('blk', 'uly')), may hold values from -4.5 to 4.5
- values: bfloat16 [4, 4096, 1024], P('section', ('blk', 'uly')), may hold values from -6 to 6
- pre_keys: bfloat16 [4, 256, 1024], P('section', ('blk', 'uly')), may hold values from -6 to 6
- pre_values: bfloat16 [4, 256, 1024], P('section', ('blk', 'uly')), may hold values from -6 to 6
- d_out: bfloat16 [4, 4096, 5120], P('section', ('blk', 'uly')), may hold values from -6 to 6
- prefix_fill: int32 [4], replicated, may hold values from 1 to 64, 192 in all
Outputs:
- next_input: bfloat16 [4, 4096, 5120], P('section', ('blk', 'uly'))
- query_grad: bfloat16 [4, 4096, 5120], P('section', ('blk', 'uly'))
- key_grad: bfloat16 [4, 4096, 1024], P('section', ('blk', 'uly'))
- value_grad: bfloat16 [4, 4096, 1024], P('section', ('blk', 'uly'))
Inputs may be any that keep to these rules, and one draw needn't show every extreme that they name: `prefix_fill`: entry b counts the live rows at the start of prefix block b of 64 rows; some block is full.
All inputs are finite; a program needn't handle non-finite values.
Results may differ from a plain program's by a relative error of at most 0.014.
Values may be sent and summed in bfloat16 or wider, within the bound.
No kernel may reach another device: no remote copies, remote signals or barrier semaphores. Data moves between devices by JAX's collectives and lax.ppermute only.
A program may use at most 128 MiB of HBM per device.

v0:
```python
import math

import jax
import jax.numpy as jnp
from jax import lax
from jax.sharding import PartitionSpec as P

HD = 128


NEG = -1e30


def shifted(block, axis, distance):
    devices = range(lax.axis_size(axis))
    route = [((i - distance) % len(devices), i) for i in devices]
    return lax.ppermute(block, axis, route)


def attend(queries, keys, values, pre_keys, pre_values, d_out, prefix_fill, first_row, kv_heads):
    rows = queries.shape[0]
    head_dim = keys.shape[1] // kv_heads
    group = queries.shape[1] // (kv_heads * head_dim)
    scale = 1.0 / math.sqrt(head_dim)
    key_rows = keys.shape[0]
    width = math.gcd(key_rows, 512)
    pre_total = pre_keys.shape[0]
    pre_block = pre_total // prefix_fill.shape[0]
    q_four = queries.reshape(rows, kv_heads, group, head_dim)
    d_four = d_out.reshape(rows, kv_heads, group, head_dim)
    pre_k = pre_keys.reshape(pre_total, kv_heads, head_dim)
    pre_v = pre_values.reshape(pre_total, kv_heads, head_dim)
    pre_index = jnp.arange(pre_total, dtype=jnp.int32)
    pre_live = pre_index % pre_block < prefix_fill[pre_index // pre_block]
    pre_mask = jnp.broadcast_to(pre_live[None, :], (rows, pre_total))
    query_pos = first_row + jnp.arange(rows, dtype=jnp.int32)
    count = (first_row + rows + width - 1) // width

    def scores(block_keys, live):
        raw = (
            jnp.einsum("rkgd,nkd->kgrn", q_four, block_keys, preferred_element_type=jnp.float32)
            * scale
        )
        return jnp.where(live[None, None], raw, NEG)

    def new_block(index):
        start = index * width
        block_keys = lax.dynamic_slice_in_dim(keys, start, width, 0).reshape(
            width, kv_heads, head_dim
        )
        block_values = lax.dynamic_slice_in_dim(values, start, width, 0).reshape(
            width, kv_heads, head_dim
        )
        live = (start + jnp.arange(width, dtype=jnp.int32))[None, :] <= query_pos[:, None]
        return (start, block_keys, block_values, live)

    def stats_step(state, block_keys, live):
        top, total = state
        score = scores(block_keys, live)
        new_top = jnp.maximum(top, jnp.max(score, axis=-1))
        terms = jnp.where(live[None, None], jnp.exp(score - new_top[..., None]), 0.0)
        total = total * jnp.exp(top - new_top) + jnp.sum(terms, axis=-1)
        return (new_top, total)

    start_stats = (
        jnp.full((kv_heads, group, rows), NEG, jnp.float32),
        jnp.zeros((kv_heads, group, rows), jnp.float32),
    )
    stats = stats_step(start_stats, pre_k, pre_mask)

    def stats_loop(index, carry):
        start, block_keys, block_values, live = new_block(index)
        return stats_step(carry, block_keys, live)

    top, total = lax.fori_loop(0, count, stats_loop, stats)
    lse = top + jnp.log(total)

    def weight_step(block_keys, block_values, live):
        score = scores(block_keys, live)
        prob = jnp.where(live[None, None], jnp.exp(score - lse[..., None]), 0.0)
        return jnp.einsum(
            "kgrn,nkd->kgrd",
            prob.astype(jnp.bfloat16),
            block_values,
            preferred_element_type=jnp.float32,
        )

    accum_start = weight_step(pre_k, pre_v, pre_mask)

    def value_loop(index, accum):
        start, block_keys, block_values, live = new_block(index)
        return accum + weight_step(block_keys, block_values, live)

    accum = lax.fori_loop(0, count, value_loop, accum_start)
    out_four = jnp.transpose(accum, (2, 0, 1, 3)).astype(jnp.bfloat16)
    delta = jnp.transpose(
        jnp.sum(d_four.astype(jnp.float32) * out_four.astype(jnp.float32), axis=-1), (1, 2, 0)
    )

    def backward_step(block_keys, block_values, live):
        score = scores(block_keys, live)
        prob = jnp.where(live[None, None], jnp.exp(score - lse[..., None]), 0.0)
        dprob = jnp.einsum(
            "rkgd,nkd->kgrn", d_four, block_values, preferred_element_type=jnp.float32
        )
        dscore = (prob * (dprob - delta[..., None]) * scale).astype(jnp.bfloat16)
        dq_part = jnp.einsum(
            "kgrn,nkd->rkgd", dscore, block_keys, preferred_element_type=jnp.float32
        )
        return (prob, dscore, dq_part)

    unused_prob, unused_score, dq_start = backward_step(pre_k, pre_v, pre_mask)
    grads_start = jnp.zeros((key_rows, 2 * kv_heads * head_dim), jnp.float32)

    def backward_loop(index, carry):
        dq_total, grads = carry
        start, block_keys, block_values, live = new_block(index)
        prob, dscore, dq_part = backward_step(block_keys, block_values, live)
        dk_part = jnp.einsum("kgrn,rkgd->nkd", dscore, q_four, preferred_element_type=jnp.float32)
        dv_part = jnp.einsum(
            "kgrn,rkgd->nkd", prob.astype(jnp.bfloat16), d_four, preferred_element_type=jnp.float32
        )
        piece = jnp.concatenate([dk_part.reshape(width, -1), dv_part.reshape(width, -1)], axis=1)
        grads = lax.dynamic_update_slice_in_dim(grads, piece, start, 0)
        return (dq_total + dq_part, grads)

    dq_total, grads = lax.fori_loop(0, count, backward_loop, (dq_start, grads_start))
    out_rows = out_four.reshape(rows, -1)
    dq_rows = dq_total.reshape(rows, -1).astype(jnp.bfloat16)
    lse_rows = jnp.transpose(lse, (2, 0, 1)).reshape(rows, -1)
    delta_rows = jnp.transpose(delta, (2, 0, 1)).reshape(rows, -1)
    return (out_rows, dq_rows, grads, lse_rows, delta_rows)


def shards(queries, keys, values, pre_keys, pre_values, d_out, prefix_fill):
    uly_size = lax.axis_size("uly")
    query_local = queries[0]
    key_local = keys[0]
    value_local = values[0]
    pk_local = pre_keys[0]
    pv_local = pre_values[0]
    d_local = d_out[0]
    kv_cols = key_local.shape[1] // uly_size
    q_heads, d_heads, k_part, v_part, pk_part, pv_part = (
        lax.all_to_all(query_local, "uly", split_axis=1, concat_axis=0, tiled=True),
        lax.all_to_all(d_local, "uly", split_axis=1, concat_axis=0, tiled=True),
        lax.all_to_all(key_local, "uly", split_axis=1, concat_axis=0, tiled=True),
        lax.all_to_all(value_local, "uly", split_axis=1, concat_axis=0, tiled=True),
        lax.all_to_all(pk_local, "uly", split_axis=1, concat_axis=0, tiled=True),
        lax.all_to_all(pv_local, "uly", split_axis=1, concat_axis=0, tiled=True),
    )
    k_heads, v_heads, pk_heads, pv_heads = (
        lax.all_gather(k_part, "blk", axis=0, tiled=True),
        lax.all_gather(v_part, "blk", axis=0, tiled=True),
        lax.all_gather(pk_part, "blk", axis=0, tiled=True),
        lax.all_gather(pv_part, "blk", axis=0, tiled=True),
    )
    block_rows = q_heads.shape[0]
    first_row = lax.axis_index("blk") * block_rows
    kv_heads = kv_cols // HD
    out_heads, dq_heads, grads, lse_rows, delta_rows = attend(
        q_heads, k_heads, v_heads, pk_heads, pv_heads, d_heads, prefix_fill, first_row, kv_heads
    )
    owned = lax.psum_scatter(
        grads.astype(jnp.bfloat16), "blk", scatter_dimension=0, tiled=True
    ).astype(jnp.float32)
    dk_heads = owned[:, :kv_cols].astype(jnp.bfloat16)
    dv_heads = owned[:, kv_cols:].astype(jnp.bfloat16)
    out_tok, dq_tok, dk_tok, dv_tok = (
        lax.all_to_all(out_heads, "uly", split_axis=0, concat_axis=1, tiled=True),
        lax.all_to_all(dq_heads, "uly", split_axis=0, concat_axis=1, tiled=True),
        lax.all_to_all(dk_heads, "uly", split_axis=0, concat_axis=1, tiled=True),
        lax.all_to_all(dv_heads, "uly", split_axis=0, concat_axis=1, tiled=True),
    )
    moved_out = shifted(out_tok[None], "section", 1)
    moved_q, moved_k, moved_v = shifted((dq_tok[None], dk_tok[None], dv_tok[None]), "section", -1)
    return (moved_out, moved_q, moved_k, moved_v)


def solution(mesh):
    return jax.shard_map(
        shards,
        mesh=mesh,
        in_specs=(
            P("section", ("blk", "uly"), None),
            P("section", ("blk", "uly"), None),
            P("section", ("blk", "uly"), None),
            P("section", ("blk", "uly"), None),
            P("section", ("blk", "uly"), None),
            P("section", ("blk", "uly"), None),
            P(),
        ),
        out_specs=(
            P("section", ("blk", "uly"), None),
            P("section", ("blk", "uly"), None),
            P("section", ("blk", "uly"), None),
            P("section", ("blk", "uly"), None),
        ),
        check_vma=False,
    )
```

profile of v0, /device:TPU:0, one launch (start us, length us, event | category | flops | bytes accessed | tf_op | source)
XLA Modules:
  0.0 481.4 jit_solution(10899290449218732948)
XLA Ops:
  7.2 15.7 %all_to_all.169 = bf16[8,8,128]{2,0,1:T(8,128)(2,1)S(1)} all-to-all(bf16[8,8,128]{2,0,1:T(8,128)(2,1)} %bitcast.398), channel_id=1, replica_groups=mesh['section'=4,'blk'=4,'uly'=8] {'uly'}, dimensions={1} | all-to-all | bytes 32768 | tf_op jit(solution)/shard_map/all_to_all | solution.py:149
  22.9 3.3 all-to-all-start.3
  28.0 5.9 %all-to-all-done.3 = bf16[8,8,128]{2,0,1:T(8,128)(2,1)S(1)} async-done(((bf16[8,8,128]{2,0,1:T(8,128)(2,1)}), bf16[8,8,128]{2,0,1:T(8,128)(2,1)S(1)}, u32[]{:S(2)}, u32[]{:S(2)}) %all-to-all-start.3) | async-done | bytes 16416 | tf_op jit(solution)/shard_map/all_to_all | solution.py:150
  33.9 3.4 all-to-all-start.2
  39.1 7.0 %all-to-all-done.2 = bf16[128,8,128]{2,0,1:T(8,128)(2,1)S(1)} async-done(((bf16[128,8,128]{2,0,1:T(8,128)(2,1)}), bf16[128,8,128]{2,0,1:T(8,128)(2,1)S(1)}, u32[]{:S(2)}, u32[]{:S(2)}) %all-to-all-start.2) | async-done | bytes 262176 | tf_op jit(solution)/shard_map/all_to_all | solution.py:147
  46.0 3.4 all-to-all-start.4
  49.5 2.4 copy.87
  51.9 6.3 %all-to-all-done.4 = bf16[128,8,128]{2,0,1:T(8,128)(2,1)S(1)} async-done(((bf16[128,8,128]{2,0,1:T(8,128)(2,1)}), bf16[128,8,128]{2,0,1:T(8,128)(2,1)S(1)}, u32[]{:S(2)}, u32[]{:S(2)}) %all-to-all-start.4) | async-done | bytes 262176 | tf_op jit(solution)/shard_map/all_to_all | solution.py:148
  58.2 3.6 all-to-all-start.1
  64.0 13.2 %all-to-all-done.1 = bf16[128,8,640]{0,2,1:T(8,128)(2,1)S(1)} async-done(((bf16[128,8,640]{0,2,1:T(8,128)(2,1)}), bf16[128,8,640]{0,2,1:T(8,128)(2,1)S(1)}, u32[]{:S(2)}, u32[]{:S(2)}) %all-to-all-start.1) | async-done | bytes 1310752 | tf_op jit(solution)/shard_map/all_to_all | solution.py:145
  77.1 4.3 all-to-all-start.6
  82.1 2.6 compare_select_fusion.1
  84.8 17.0 %all_gather.14 = bf16[256,128]{1,0:T(8,128)(2,1)S(1)} all-gather(bf16[64,128]{1,0:T(8,128)(2,1)S(1)} %bitcast.389), channel_id=1, replica_groups=mesh['section'=4,'blk'=4,'uly'=8] {'blk'}, dimensions={0}, use_global_device_ids=true | all-gather | bytes 81920 | tf_op jit(solution)/shard_map/all_gather | solution.py:156
  101.8 5.2 %all_gather.12 = bf16[256,128]{1,0:T(8,128)(2,1)S(1)} all-gather(bf16[64,128]{1,0:T(8,128)(2,1)S(1)} %bitcast.388), channel_id=1, replica_groups=mesh['section'=4,'blk'=4,'uly'=8] {'blk'}, dimensions={0}, use_global_device_ids=true | all-gather | bytes 81920 | tf_op jit(solution)/shard_map/all_gather | solution.py:155
  115.8 2.4 bitcast_reduce_fusion
  122.1 12.2 %while.37 = (s32[]{:T(128)}, f32[1,5,1024]{2,1,0:T(8,128)S(1)}, f32[1,5,1024]{2,1,0:T(8,128)S(1)}, s32[]{:T(128)}, bf16[4096,128]{1,0:T(8,128)(2,1)}, /*index=5*...) while((s32[]{:T(128)}, f32[1,5,1024]{2,1,0:T(8,128)S(1)}, ...), condition=%wide.region_5.6_spmd.clone, body=%wide.region_2.5_spmd.clone.sunk | while | flops 692596224 | bytes 24264872 | solution.py:75
  123.0 2.8 fusion.145
  125.8 2.5 select_reduce_fusion.2
  128.8 2.8 fusion.145
  131.7 2.5 select_reduce_fusion.2
  134.3 5.9 %fusion.100 = f32[1,5,1024,128]{3,2,1,0:T(8,128)} fusion(f32[256,1024,5]{1,0,2:T(8,128)} %copy-done.3, f32[5,1024]{1,0:T(8,128)S(1)} %bitcast.390, pred[256]{0:T(512)(128)(4,1)S(1)} %fusion.112, bf16[256,128]{1,0:T(8,128)(2,1)S(1)} %all_gather.14), kind=kOutput, calls=%fused_computation.104 | convolution fusion | flops 342097920 | bytes 7950592 | tf_op jit(solution)/shard_map/kgrn,nkd->kgrd/dot_general | solution.py:81
  140.2 16.6 %while.38 = (s32[]{:T(128)}, f32[1,5,1024,128]{3,2,1,0:T(8,128)}, s32[]{:T(128)}, bf16[4096,128]{1,0:T(8,128)(2,1)}, bf16[1024,1,5,128]{3,0,2,1:T(8,128)(2,1)S(1...) while((s32[]{:T(128)}, f32[1,5,1024,128]{3,2,1,0:T(8,128)}, ...), condition=%wide.region_7.8_spmd.clone, body=%wide.region_6.7_spmd.clone.sunk | while | flops 1356465664 | bytes 7898283 | solution.py:94
  140.6 7.8 %bitcast_add_fusion.8 = f32[1,5,1024,128]{3,2,1,0:T(8,128)} fusion(f32[1,5,1024,128]{3,2,1,0:T(8,128)} %get-tuple-element.598, f32[5,1024]{1,0:T(8,128)S(1)} %bitcast.391, pred[1024,512]{0,1:T(8,128)(4,1)S(1)} %broadcast_compare_fusion.7, bf16[1024,1,5,128]{3,0,2,1:T(8,128)(2,1)S(1)} %get-tuple-element.613, ...), kind=kOutput, calls=%fused_computation.25.clone.1 | convolution fusion | flops 1355939840 | bytes 7361536 | tf_op jit(solution)/shard_map/while/body/kgrn,nkd->kgrd/dot_general | solution.py:81
  148.8 7.8 %bitcast_add_fusion.8 = f32[1,5,1024,128]{3,2,1,0:T(8,128)} fusion(f32[1,5,1024,128]{3,2,1,0:T(8,128)} %get-tuple-element.598, f32[5,1024]{1,0:T(8,128)S(1)} %bitcast.391, pred[1024,512]{0,1:T(8,128)(4,1)S(1)} %broadcast_compare_fusion.7, bf16[1024,1,5,128]{3,0,2,1:T(8,128)(2,1)S(1)} %get-tuple-element.613, ...), kind=kOutput, calls=%fused_computation.25.clone.1 | convolution fusion | flops 1355939840 | bytes 7361536 | tf_op jit(solution)/shard_map/while/body/kgrn,nkd->kgrd/dot_general | solution.py:81
  161.1 7.4 %fusion.103 = f32[1024,1,5,128]{3,0,2,1:T(8,128)} fusion(f32[256,1024,5]{1,0,2:T(8,128)} %copy-done.3, f32[5,1024]{1,0:T(8,128)S(1)} %bitcast.395, f32[5,1024]{1,0:T(8,128)S(1)} %bitcast.392, pred[256]{0:T(512)(128)(4,1)S(1)} %fusion.112, bf16[1024,5,128]{0,2,1:T(8,128)(2,1)} %reshape.366, bf16[256,128]{1,0:T(8,128)(2,1)S(1)} %all_gather.14, ...), kind=kOutput, calls=%fused_computation.105 | convolution fusion | flops 681574400 | bytes 9347328 | tf_op jit(solution)/shard_map/kgrn,nkd->rkgd/dot_general | solution.py:107
  168.4 3.3 copy.104
  173.3 34.3 %while.39 = (s32[]{:T(128)}, f32[1024,1,5,128]{0,3,2,1:T(8,128)}, bf16[4096,256]{0,1:T(8,128)(2,1)}, s32[]{:T(128)}, bf16[4096,128]{1,0:T(8,128)(2,1)}, /*index=...) while((s32[]{:T(128)}, f32[1024,1,5,128]{0,3,2,1:T(8,128)}, ...), condition=%wide.region_10.11_spmd.clone, body=%wide.region_9.10_spmd.clone.sunk | while | flops 3391227392 | bytes 86712608 | solution.py:127
  173.7 2.5 fusion.160
  176.2 3.3 fusion.162
  179.5 5.2 %fusion.161 = bf16[5,1024,512]{1,2,0:T(8,128)(2,1)S(1)} fusion(f32[512,1024,5]{1,0,2:T(8,128)S(1)} %fusion.160, f32[5,1024]{1,0:T(8,128)S(1)} %bitcast.397, f32[5,1024]{1,0:T(8,128)S(1)} %bitcast.394, pred[1024,512]{0,1:T(8,128)(4,1)S(1)} %broadcast_compare_fusion.8, bf16[1024,1,5,128]{0,3,2,1:T(8,128)(2,1)S(1)} %copy-done.5, ...), kind=kOutput, calls=%fused_computation.48.clone.1 | convolution fusion | flops 692060160 | bytes 17735684 | tf_op jit(solution)/shard_map/while/body/rkgd,nkd->kgrn/dot_general | solution.py:103
  190.7 2.5 fusion.160
  193.3 3.3 fusion.162
  196.6 5.2 %fusion.161 = bf16[5,1024,512]{1,2,0:T(8,128)(2,1)S(1)} fusion(f32[512,1024,5]{1,0,2:T(8,128)S(1)} %fusion.160, f32[5,1024]{1,0:T(8,128)S(1)} %bitcast.397, f32[5,1024]{1,0:T(8,128)S(1)} %bitcast.394, pred[1024,512]{0,1:T(8,128)(4,1)S(1)} %broadcast_compare_fusion.8, bf16[1024,1,5,128]{0,3,2,1:T(8,128)(2,1)S(1)} %copy-done.5, ...), kind=kOutput, calls=%fused_computation.48.clone.1 | convolution fusion | flops 692060160 | bytes 17735684 | tf_op jit(solution)/shard_map/while/body/rkgd,nkd->kgrn/dot_general | solution.py:103
  207.6 2.9 copy.129
  210.5 2.8 copy.97
  213.3 6.5 %all-to-all-start.5 = ((bf16[8,128,640]{2,1,0:T(8,128)(2,1)}), bf16[8,128,640]{2,1,0:T(8,128)(2,1)}, u32[]{:S(2)}, u32[]{:S(2)}) async-start(bf16[8,128,640]{2,1,0:T(8,128)(2,1)} %copy.97), calls=%async_computation.5 | async-start | bytes 2621440 | tf_op jit(solution)/shard_map/all_to_all | solution.py:170
  222.3 12.0 %all-to-all-done.5 = bf16[8,128,640]{2,1,0:T(8,128)(2,1)} async-done(((bf16[8,128,640]{2,1,0:T(8,128)(2,1)}), bf16[8,128,640]{2,1,0:T(8,128)(2,1)}, u32[]{:S(2)}, u32[]{:S(2)}) %all-to-all-start.5) | async-done | bytes 1310752 | tf_op jit(solution)/shard_map/all_to_all | solution.py:170
  234.3 3.6 all-to-all-start.7
  241.2 11.0 %all-to-all-done.7 = bf16[8,128,640]{2,1,0:T(8,128)(2,1)S(1)} async-done(((bf16[8,128,640]{2,1,0:T(8,128)(2,1)}), bf16[8,128,640]{2,1,0:T(8,128)(2,1)S(1)}, u32[]{:S(2)}, u32[]{:S(2)}) %all-to-all-start.7) | async-done | bytes 1310752 | tf_op jit(solution)/shard_map/all_to_all | solution.py:171
  253.7 2.8 collective-permute-start.1
  256.4 177.8 %reduce-scatter.2.cloned.1.call-done = bf16[1024,256]{0,1:T(8,128)(2,1)} async-done(((bf16[4096,256]{0,1:T(8,128)(2,1)}), bf16[1024,256]{0,1:T(8,128)(2,1)}) %reduce-scatter.2.cloned.1.call-update) | async-done | bytes 524304 | tf_op jit(solution)/shard_map/reduce_scatter | solution.py:164
  436.2 7.9 %all-to-all-start.8 = ((bf16[8,128,128]{2,1,0:T(8,128)(2,1)}), bf16[8,128,128]{2,1,0:T(8,128)(2,1)S(1)}, u32[]{:S(2)}, u32[]{:S(2)}) async-start(bf16[8,128,128]{2,1,0:T(8,128)(2,1)} %bitcast.42), calls=%async_computation.9 | async-start | bytes 524288 | tf_op jit(solution)/shard_map/all_to_all | solution.py:172
  444.9 8.4 %all-to-all-done.8 = bf16[8,128,128]{2,1,0:T(8,128)(2,1)S(1)} async-done(((bf16[8,128,128]{2,1,0:T(8,128)(2,1)}), bf16[8,128,128]{2,1,0:T(8,128)(2,1)S(1)}, u32[]{:S(2)}, u32[]{:S(2)}) %all-to-all-start.8) | async-done | bytes 262176 | tf_op jit(solution)/shard_map/all_to_all | solution.py:172
  453.3 3.4 all-to-all-start.9
  456.9 2.7 collective-permute-start.2
  459.6 6.0 %all-to-all-done.9 = bf16[8,128,128]{2,1,0:T(8,128)(2,1)S(1)} async-done(((bf16[8,128,128]{2,1,0:T(8,128)(2,1)}), bf16[8,128,128]{2,1,0:T(8,128)(2,1)S(1)}, u32[]{:S(2)}, u32[]{:S(2)}) %all-to-all-start.9) | async-done | bytes 262176 | tf_op jit(solution)/shard_map/all_to_all | solution.py:173
  466.4 2.6 collective-permute-start.3
  469.0 2.4 copy.111
  (104 shorter events, 52.6 us)
Async XLA Ops:
  7.2 55.4 %copy-start.6 = (bf16[1,128,5120]{2,1,0:T(8,128)(2,1)S(1)}, bf16[1,128,5120]{2,1,0:T(8,128)(2,1)}, u32[]{:S(2)}) copy-start(bf16[1,128,5120]{2,1,0:T(8,128)(2,1)} %param.18) | copy-start | bytes 3932164
  22.9 11.0 %all-to-all-start.3 = ((bf16[8,8,128]{2,0,1:T(8,128)(2,1)}), bf16[8,8,128]{2,0,1:T(8,128)(2,1)S(1)}, u32[]{:S(2)}, u32[]{:S(2)}) async-start(bf16[8,8,128]{2,0,1:T(8,128)(2,1)} %bitcast.399), calls=%async_computation.3 | async-start | bytes 32768 | tf_op jit(solution)/shard_map/all_to_all | solution.py:150
  33.9 12.1 %all-to-all-start.2 = ((bf16[128,8,128]{2,0,1:T(8,128)(2,1)}), bf16[128,8,128]{2,0,1:T(8,128)(2,1)S(1)}, u32[]{:S(2)}, u32[]{:S(2)}) async-start(bf16[128,8,128]{2,0,1:T(8,128)(2,1)} %copy.90), calls=%async_computation.2 | async-start | bytes 524288 | tf_op jit(solution)/shard_map/all_to_all | solution.py:147
  46.0 15.8 %copy-start.8 = (bf16[128,8,128]{2,0,1:T(8,128)(2,1)}, bf16[128,8,128]{2,0,1:T(8,128)(2,1)S(1)}, u32[]{:S(2)}) copy-start(bf16[128,8,128]{2,0,1:T(8,128)(2,1)S(1)} %all-to-all-done.2) | copy-start | bytes 786436
  46.0 12.1 %all-to-all-start.4 = ((bf16[128,8,128]{2,0,1:T(8,128)(2,1)}), bf16[128,8,128]{2,0,1:T(8,128)(2,1)S(1)}, u32[]{:S(2)}, u32[]{:S(2)}) async-start(bf16[128,8,128]{2,0,1:T(8,128)(2,1)} %copy.94), calls=%async_computation.4 | async-start | bytes 524288 | tf_op jit(solution)/shard_map/all_to_all | solution.py:148
  49.5 32.0 %copy-start.9 = (s32[4]{0:T(128)S(1)}, s32[4]{0:T(128)}, u32[]{:S(2)}) copy-start(s32[4]{0:T(128)} %param.19) | copy-start | bytes 52
  58.2 48.8 %copy-start.7 = (bf16[128,8,128]{2,0,1:T(8,128)(2,1)}, bf16[128,8,128]{2,0,1:T(8,128)(2,1)S(1)}, u32[]{:S(2)}) copy-start(bf16[128,8,128]{2,0,1:T(8,128)(2,1)S(1)} %all-to-all-done.4) | copy-start | bytes 786436
  58.2 18.9 %all-to-all-start.1 = ((bf16[128,8,640]{0,2,1:T(8,128)(2,1)}), bf16[128,8,640]{0,2,1:T(8,128)(2,1)S(1)}, u32[]{:S(2)}, u32[]{:S(2)}) async-start(bf16[128,8,640]{0,2,1:T(8,128)(2,1)} %bitcast.9), calls=%async_computation.1 | async-start | bytes 2621440 | tf_op jit(solution)/shard_map/all_to_all | solution.py:145
  61.8 60.3 %all-gather.3.cloned.1.call-start = ((), (), s32[]{:S(2)}) async-start(), calls=%async_computation.11 | async-start | bytes 1310720 | tf_op jit(solution)/shard_map/all_gather | solution.py:153
  77.1 32.9 %all-to-all-start.6 = ((bf16[128,8,640]{0,2,1:T(8,128)(2,1)}), bf16[128,8,640]{0,2,1:T(8,128)(2,1)}, u32[]{:S(2)}, u32[]{:S(2)}) async-start(bf16[128,8,640]{0,2,1:T(8,128)(2,1)} %bitcast.29), calls=%async_computation.6 | async-start | bytes 2621440 | tf_op jit(solution)/shard_map/all_to_all | solution.py:146
  81.4 58.8 %all-gather.5.cloned.1.call-start = ((), (), s32[]{:S(2)}) async-start(), calls=%async_computation.12 | async-start | bytes 1310720 | tf_op jit(solution)/shard_map/all_gather | solution.py:154
  107.1 327.2 %reduce-scatter.2.cloned.1.call-start = ((), (), s32[]{:S(2)}) async-start(), calls=%async_computation.13 | async-start | bytes 2621440 | tf_op jit(solution)/shard_map/reduce_scatter | solution.py:164
  118.2 2.3 copy-start.3
  158.8 9.6 %copy-start.4 = (bf16[1,5,1024,128]{2,3,1,0:T(8,128)(2,1)}, bf16[1,5,1024,128]{2,3,1,0:T(8,128)(2,1)S(1)}, u32[]{:S(2)}) copy-start(bf16[1,5,1024,128]{2,3,1,0:T(8,128)(2,1)S(1)} %copy.96) | copy-start | bytes 3932164
  173.7 2.5 copy-start.5
  184.7 1.9 copy-start
  188.8 1.6 copy-start.1
  190.7 2.5 copy-start.5
  201.7 1.9 copy-start
  205.8 1.6 copy-start.1
  207.6 12.2 %copy-start.2 = (f32[1024,1,5,128]{0,3,2,1:T(8,128)S(1)}, f32[1024,1,5,128]{0,3,2,1:T(8,128)}, u32[]{:S(2)}) copy-start(f32[1024,1,5,128]{0,3,2,1:T(8,128)} %get-tuple-element.148) | copy-start | bytes 7864324
  213.3 21.0 %all-to-all-start.5 = ((bf16[8,128,640]{2,1,0:T(8,128)(2,1)}), bf16[8,128,640]{2,1,0:T(8,128)(2,1)}, u32[]{:S(2)}, u32[]{:S(2)}) async-start(bf16[8,128,640]{2,1,0:T(8,128)(2,1)} %copy.97), calls=%async_computation.5 | async-start | bytes 2621440 | tf_op jit(solution)/shard_map/all_to_all | solution.py:170
  234.3 17.9 %all-to-all-start.7 = ((bf16[8,128,640]{2,1,0:T(8,128)(2,1)}), bf16[8,128,640]{2,1,0:T(8,128)(2,1)S(1)}, u32[]{:S(2)}, u32[]{:S(2)}) async-start(bf16[8,128,640]{2,1,0:T(8,128)(2,1)} %copy.105), calls=%async_computation.7 | async-start | bytes 2621440 | tf_op jit(solution)/shard_map/all_to_all | solution.py:171
  239.6 229.4 %collective-permute-start = (bf16[1,128,5120]{1,2,0:T(8,128)(2,1)S(1)}, bf16[1,128,5120]{1,2,0:T(8,128)(2,1)}, u32[]{:S(2)}, u32[]{:S(2)}) collective-permute-start(bf16[1,128,5120]{1,2,0:T(8,128)(2,1)S(1)} %bitcast.378), channel_id=1, source_target_pairs={{96,0},{0,32},{32,64},{64,96},{97,1},{1,33},{33,65},{65,97},{98,2}... | collective-permute-start | bytes 3932168 | tf_op jit(solution)/shard_map/ppermute | solution.py:17
  253.7 217.8 %collective-permute-start.1 = (bf16[1,128,5120]{1,2,0:T(8,128)(2,1)}, bf16[1,128,5120]{1,2,0:T(8,128)(2,1)S(1)}, u32[]{:S(2)}, u32[]{:S(2)}) collective-permute-start(bf16[1,128,5120]{1,2,0:T(8,128)(2,1)} %bitcast.379), channel_id=1, source_target_pairs={{32,0},{64,32},{96,64},{0,96},{33,1},{65,33},{97,65},{1,97},{34,2}... | collective-permute-start | bytes 3932168 | tf_op jit(solution)/shard_map/ppermute | solution.py:17
  436.2 17.1 %all-to-all-start.8 = ((bf16[8,128,128]{2,1,0:T(8,128)(2,1)}), bf16[8,128,128]{2,1,0:T(8,128)(2,1)S(1)}, u32[]{:S(2)}, u32[]{:S(2)}) async-start(bf16[8,128,128]{2,1,0:T(8,128)(2,1)} %bitcast.42), calls=%async_computation.9 | async-start | bytes 524288 | tf_op jit(solution)/shard_map/all_to_all | solution.py:172
  453.3 12.3 %all-to-all-start.9 = ((bf16[8,128,128]{2,1,0:T(8,128)(2,1)}), bf16[8,128,128]{2,1,0:T(8,128)(2,1)S(1)}, u32[]{:S(2)}, u32[]{:S(2)}) async-start(bf16[8,128,128]{2,1,0:T(8,128)(2,1)} %bitcast.45), calls=%async_computation.10 | async-start | bytes 524288 | tf_op jit(solution)/shard_map/all_to_all | solution.py:173
  456.9 16.0 %collective-permute-start.2 = (bf16[1,128,1024]{1,2,0:T(8,128)(2,1)S(1)}, bf16[1,128,1024]{1,2,0:T(8,128)(2,1)S(1)}, u32[]{:S(2)}, u32[]{:S(2)}) collective-permute-start(bf16[1,128,1024]{1,2,0:T(8,128)(2,1)S(1)} %bitcast.386), channel_id=1, source_target_pairs={{32,0},{64,32},{96,64},{0,96},{33,1},{65,33},{97,65},{1,97},{34,2}... | collective-permute-start | bytes 786440 | tf_op jit(solution)/shard_map/ppermute | solution.py:17
  466.4 7.4 %collective-permute-start.3 = (bf16[1,128,1024]{1,2,0:T(8,128)(2,1)}, bf16[1,128,1024]{1,2,0:T(8,128)(2,1)S(1)}, u32[]{:S(2)}, u32[]{:S(2)}) collective-permute-start(bf16[1,128,1024]{1,2,0:T(8,128)(2,1)} %bitcast.387), channel_id=1, source_target_pairs={{32,0},{64,32},{96,64},{0,96},{33,1},{65,33},{97,65},{1,97},{34,2}... | collective-permute-start | bytes 786440 | tf_op jit(solution)/shard_map/ppermute | solution.py:17
Sparse Core Ops, SparseCore 0:
  64.9 36.6 all-gather.2
  107.2 21.6 all-gather.4
  207.8 226.4 reduce-scatter.1
where the time goes:
time: 490 us; the launch traced here: 481 us
  waiting for transfers between devices  248 us (51%)
  matrix products  67 us (14%)
  starting transfers between devices  49.1 us (10%)
  local copies, waits for them, and re-layouts  48 us (10%)
  blocking collectives  38 us (8%)
  other arithmetic  15.6 us (3%)
  between operations  14.3 us (3%)
    reduce_scatter x1, waiting for transfers between devices, shards(): lax.psum_scatter(grads.astype(jnp.bfloat16), 'blk', scatter_dimension=0,...  178 us
    dot_general x3, matrix products, weight_step(): jnp.einsum('kgrn,nkd->kgrd', prob.astype(jnp.bfloat16), block_values, pre...  21.6 us
    unnamed x26, local copies, waits for them, and re-layouts  21 us
    all_gather x1, blocking collectives, shards(): lax.all_gather(pv_part, 'blk', axis=0, tiled=True)  17 us
    all_to_all x1, blocking collectives, shards(): lax.all_to_all(pk_local, 'uly', split_axis=1, concat_axis=0, tiled=True)  15.7 us
    all_to_all x1, waiting for transfers between devices, shards(): lax.all_to_all(query_local, 'uly', split_axis=1, concat_axis=0, tiled=True)  13.2 us
    dot_general x5, matrix products, scores(): jnp.einsum('rkgd,nkd->kgrn', q_four, block_keys, preferred_element_type=j...  13.1 us
    all_to_all x1, waiting for transfers between devices, shards(): lax.all_to_all(out_heads, 'uly', split_axis=0, concat_axis=1, tiled=True)  12 us
  transfers between devices with their start and end apart: 16, of which 9 were waited for; matrix products, arithmetic and copies ran while one was open for 13% of the time, Pallas kernels for 0%

commit v1 on v0

v1 whole, which is shorter than its diff:
```python
import math

import jax
import jax.numpy as jnp
import numpy as np
from jax import lax
from jax.experimental import pallas as pl
from jax.experimental.pallas import tpu as pltpu
from jax.sharding import PartitionSpec as P

HD = 128
GROUP = 5
CHUNKS = 32
TOK = 128
SPLIT = 4
SUB = TOK // SPLIT
QR = GROUP * SUB
PRE = 8
K0, V0, P0 = QR, QR + TOK, QR + 2 * TOK
PACK = P0 + 2 * PRE
RC = 8
KC = 4
M = RC * QR
N = KC * TOK
N_RB = CHUNKS // RC
PTOT = CHUNKS * PRE
SCALE = 1.0 / math.sqrt(HD)
SAFE = 60.0
NEG = -1e30
F32 = jnp.float32
BF16 = jnp.bfloat16
VMEM = 60 * 2**20

ROW_OF = np.array([r for r in range(N_RB) for _ in range(2 * r + 2)], np.int32)
KEY_OF = np.array([k for r in range(N_RB) for k in range(2 * r + 2)], np.int32)
STEPS = len(ROW_OF)


def dot(a, b, ca, cb):
    return lax.dot_general(a, b, (((ca,), (cb,)), ((), ())), preferred_element_type=F32)


def wide(x, width):
    return jnp.concatenate([x] * (width // x.shape[1]), axis=1)


def row_pos(first_chunk, chunks, width, part):
    shape = (chunks, GROUP, SUB, width)
    pos = lax.broadcasted_iota(jnp.int32, shape, 0) * TOK + lax.broadcasted_iota(jnp.int32, shape, 2)
    return pos.reshape(chunks * QR, width) + (first_chunk * TOK + part * SUB)


def key_pos(rows, width):
    return lax.broadcasted_iota(jnp.int32, (rows, width), 1)


def prefix_live(fill_ref, rows):
    pos = key_pos(rows, PTOT)
    live = pos < 0
    block = PTOT // SPLIT
    for b in range(SPLIT):
        live = live | ((pos >= b * block) & (pos < b * block + fill_ref[b]))
    return live


def prefix_rows(pack_ref, which):
    both = pack_ref[:, P0:PACK, :].astype(F32)
    return both[:, which * PRE : (which + 1) * PRE].reshape(PTOT, HD).astype(BF16)


def sub_tiles(kind, part):
    def tri(chunk, chunks, width, key_first):
        pos = row_pos(chunk, chunks, width, part)
        return key_pos(chunks * QR, width) + key_first <= pos

    if kind == "full":
        return [(0, M, N, lambda: None)]
    if kind == "first":
        return [
            (0, 2 * QR, N // 2, lambda: tri(0, 2, N // 2, 0)),
            (2 * QR, 4 * QR, N, lambda: tri(2, 2, N, 0)),
            (4 * QR, M, N, lambda: None),
        ]
    return [
        (4 * QR, 6 * QR, N // 2, lambda: tri(4, 2, N // 2, N)),
        (6 * QR, M, N, lambda: tri(6, 2, N, N)),
    ]


def forward_kernel(row_of, key_of, meta, pack, e_out, ep_out, o_out, li_out, acc, shift, pk, pv, knorm):
    t = pl.program_id(0)
    rb, kb = row_of[t], key_of[t]
    part = meta[SPLIT]

    @pl.when(t == 0)
    def _():
        pk[...] = prefix_rows(pack, 0)
        pv[...] = prefix_rows(pack, 1)
        top = jnp.max(jnp.sum(jnp.square(pk[...].astype(F32)), axis=1))

        def step(c, best):
            rows = pack[c, K0:V0, :].astype(F32)
            return jnp.maximum(best, jnp.max(jnp.sum(rows * rows, axis=1)))

        knorm[0] = lax.fori_loop(0, CHUNKS, step, top)

    def queries():
        return pack[pl.ds(rb * RC, RC), 0:QR, :].reshape(M, HD)

    @pl.when(kb == 0)
    def _():
        acc[...] = jnp.zeros_like(acc)
        shift[...] = jnp.zeros_like(shift)
        q = queries()
        qf = q.astype(F32)
        qnorm = jnp.max(jnp.sum(qf * qf, axis=1))

        @pl.when(jnp.logical_not(qnorm * knorm[0] * (SCALE * SCALE) <= SAFE * SAFE))
        def _():
            live = prefix_live(meta, M)
            s = jnp.where(live, dot(q, pk[...], 1, 1) * SCALE, NEG)
            shift[...] = jnp.broadcast_to(jnp.max(s, axis=1, keepdims=True), shift.shape)

            def step(k, carry):
                keys = pack[pl.ds(k * KC, KC), K0:V0, :].reshape(N, HD)
                pos = row_pos(0, RC, N, part) + rb * (RC * TOK)
                s = jnp.where(key_pos(M, N) + k * N <= pos, dot(q, keys, 1, 1) * SCALE, NEG)
                top = jnp.broadcast_to(jnp.max(s, axis=1, keepdims=True), shift.shape)
                shift[...] = jnp.maximum(shift[...], top)
                return carry

            lax.fori_loop(0, 2 * rb + 2, step, 0)

    def tile(first, last, keys, values, live, store):
        width = keys.shape[0]
        q = pack[pl.ds(rb * RC + first // QR, (last - first) // QR), 0:QR, :].reshape(last - first, HD)
        s = dot(q, keys, 1, 1) * SCALE - wide(shift[first:last, :], width)
        e = jnp.exp(s)
        if live is not None:
            e = jnp.where(live, e, 0.0)
        e = e.astype(BF16)
        store[0, first:last, 0:width] = e
        both = jnp.concatenate([values, jnp.ones_like(values)], axis=1)
        acc[first:last, :] += dot(e, both, 1, 0)

    keys = lambda n: pack[pl.ds(kb * KC, n // TOK), K0:V0, :].reshape(n, HD)
    values = lambda n: pack[pl.ds(kb * KC, n // TOK), V0:P0, :].reshape(n, HD)

    @pl.when(kb < 2 * rb)
    def _():
        for first, last, n, live in sub_tiles("full", part):
            tile(first, last, keys(n), values(n), live(), e_out)

    @pl.when(kb == 2 * rb)
    def _():
        for first, last, n, live in sub_tiles("first", part):
            tile(first, last, keys(n), values(n), live(), e_out)

    @pl.when(kb == 2 * rb + 1)
    def _():
        for first, last, n, live in sub_tiles("second", part):
            tile(first, last, keys(n), values(n), live(), e_out)
        tile(0, M, pk[...], pv[...], prefix_live(meta, M), ep_out)
        inverse = 1.0 / acc[:, HD:]
        li_out[...] = inverse
        o_out[...] = (acc[:, :HD] * inverse).astype(BF16).reshape(RC, QR, HD)


def forward(meta, pack):
    whole = lambda *shape: pl.BlockSpec(shape, lambda t, r, k, m: (0,) * len(shape))
    return pl.pallas_call(
        forward_kernel,
        grid_spec=pltpu.PrefetchScalarGridSpec(
            num_scalar_prefetch=3,
            grid=(STEPS,),
            in_specs=[whole(CHUNKS, PACK, HD)],
            out_specs=[
                pl.BlockSpec((1, M, N), lambda t, r, k, m: (t, 0, 0)),
                pl.BlockSpec((1, M, PTOT), lambda t, r, k, m: (r[t], 0, 0)),
                pl.BlockSpec((RC, QR, HD), lambda t, r, k, m: (r[t], 0, 0)),
                pl.BlockSpec((M, HD), lambda t, r, k, m: (r[t], 0)),
            ],
            scratch_shapes=[
                pltpu.VMEM((M, 2 * HD), F32),
                pltpu.VMEM((M, HD), F32),
                pltpu.VMEM((PTOT, HD), BF16),
                pltpu.VMEM((PTOT, HD), BF16),
                pltpu.SMEM((1,), F32),
            ],
        ),
        out_shape=[
            jax.ShapeDtypeStruct((STEPS, M, N), BF16),
            jax.ShapeDtypeStruct((N_RB, M, PTOT), BF16),
            jax.ShapeDtypeStruct((CHUNKS, QR, HD), BF16),
            jax.ShapeDtypeStruct((N_RB * M, HD), F32),
        ],
        compiler_params=pltpu.CompilerParams(vmem_limit_bytes=VMEM),
        name="forward",
    )(jnp.asarray(ROW_OF), jnp.asarray(KEY_OF), meta, pack)


def backward_kernel(row_of, key_of, meta, pack, d_in, e_in, ep_in, o_in, li_in, dq_out, dkv_out, dq, dk, dv, dn, delta, pk, pv):
    t = pl.program_id(0)
    rb, kb = row_of[t], key_of[t]
    part = meta[SPLIT]

    @pl.when(t == 0)
    def _():
        pk[...] = prefix_rows(pack, 0)
        pv[...] = prefix_rows(pack, 1)
        dk[...] = jnp.zeros_like(dk)
        dv[...] = jnp.zeros_like(dv)

    @pl.when(kb == 0)
    def _():
        dq[...] = jnp.zeros_like(dq)
        d = d_in[...].reshape(M, HD).astype(F32) * (li_in[...] * SCALE)
        d = d.astype(BF16)
        dn[...] = d
        total = jnp.sum(d.astype(F32) * o_in[...].reshape(M, HD).astype(F32), axis=1, keepdims=True)
        delta[...] = jnp.broadcast_to(total, delta.shape)

    def tile(first, last, keys, values, e_ref, grads):
        width = keys.shape[0]
        q = pack[pl.ds(rb * RC + first // QR, (last - first) // QR), 0:QR, :].reshape(last - first, HD)
        d = dn[first:last, :]
        e = e_ref[0, first:last, 0:width]
        dp = dot(d, values, 1, 1) - wide(delta[first:last, :], width)
        ds = (e.astype(F32) * dp).astype(BF16)
        dq[first:last, :] += dot(ds, keys, 1, 0)
        if grads:
            at = pl.ds(kb * N, width)
            dv[at, :] += dot(e, d, 0, 0)
            dk[at, :] += dot(ds, q, 0, 0)

    keys = lambda n: pack[pl.ds(kb * KC, n // TOK), K0:V0, :].reshape(n, HD)
    values = lambda n: pack[pl.ds(kb * KC, n // TOK), V0:P0, :].reshape(n, HD)

    @pl.when(kb < 2 * rb)
    def _():
        for first, last, n, live in sub_tiles("full", part):
            tile(first, last, keys(n), values(n), e_in, True)

    @pl.when(kb == 2 * rb)
    def _():
        for first, last, n, live in sub_tiles("first", part):
            tile(first, last, keys(n), values(n), e_in, True)

    @pl.when(kb == 2 * rb + 1)
    def _():
        for first, last, n, live in sub_tiles("second", part):
            tile(first, last, keys(n), values(n), e_in, True)
        tile(0, M, pk[...], pv[...], ep_in, False)
        dq_out[...] = dq[...].astype(BF16).reshape(RC, QR, HD)

    @pl.when(t == STEPS - 1)
    def _():
        dkv_out[:, 0:TOK, :] = dk[...].astype(BF16).reshape(CHUNKS, TOK, HD)
        dkv_out[:, TOK:, :] = (dv[...] * (1.0 / SCALE)).astype(BF16).reshape(CHUNKS, TOK, HD)


def backward(meta, pack, d, e, ep, o, li):
    whole = lambda *shape: pl.BlockSpec(shape, lambda t, r, k, m: (0,) * len(shape))
    by_rows = lambda *shape: pl.BlockSpec(shape, lambda t, r, k, m: (r[t],) + (0,) * (len(shape) - 1))
    return pl.pallas_call(
        backward_kernel,
        grid_spec=pltpu.PrefetchScalarGridSpec(
            num_scalar_prefetch=3,
            grid=(STEPS,),
            in_specs=[
                whole(CHUNKS, PACK, HD),
                by_rows(RC, QR, HD),
                pl.BlockSpec((1, M, N), lambda t, r, k, m: (t, 0, 0)),
                by_rows(1, M, PTOT),
                by_rows(RC, QR, HD),
                by_rows(M, HD),
            ],
            out_specs=[by_rows(RC, QR, HD), whole(CHUNKS, 2 * TOK, HD)],
            scratch_shapes=[
                pltpu.VMEM((M, HD), F32),
                pltpu.VMEM((CHUNKS * TOK, HD), F32),
                pltpu.VMEM((CHUNKS * TOK, HD), F32),
                pltpu.VMEM((M, HD), BF16),
                pltpu.VMEM((M, HD), F32),
                pltpu.VMEM((PTOT, HD), BF16),
                pltpu.VMEM((PTOT, HD), BF16),
            ],
        ),
        out_shape=[
            jax.ShapeDtypeStruct((CHUNKS, QR, HD), BF16),
            jax.ShapeDtypeStruct((CHUNKS, 2 * TOK, HD), BF16),
        ],
        compiler_params=pltpu.CompilerParams(vmem_limit_bytes=VMEM),
        name="backward",
    )(jnp.asarray(ROW_OF), jnp.asarray(KEY_OF), meta, pack, d, e, ep, o, li)


def to_groups(x):
    x = x.reshape(SPLIT, SUB, -1, GROUP, HD)
    return jnp.transpose(x, (0, 2, 3, 1, 4)).reshape(CHUNKS, QR, HD)


def to_tokens(x):
    x = x.reshape(SPLIT, -1, GROUP, SUB, HD)
    return jnp.transpose(x, (0, 3, 1, 2, 4)).reshape(TOK, -1)


def key_groups(x):
    rows = x.shape[0]
    x = jnp.transpose(x.reshape(rows, -1, HD), (1, 0, 2))
    return jnp.broadcast_to(x[None], (SPLIT,) + x.shape).reshape(CHUNKS, rows, HD)


def exchange(x):
    return lax.all_to_all(x, ("blk", "uly"), split_axis=0, concat_axis=0, tiled=True)


def shifted(block, distance):
    count = lax.axis_size("section")
    return lax.ppermute(block, "section", [((i - distance) % count, i) for i in range(count)])


def shards(queries, keys, values, pre_keys, pre_values, d_out, prefix_fill):
    part = lax.axis_index("blk").astype(jnp.int32)
    meta = jnp.concatenate([prefix_fill, part[None]])
    sent = jnp.concatenate(
        [to_groups(queries[0])] + [key_groups(x[0]) for x in (keys, values, pre_keys, pre_values)], axis=1
    )
    pack = exchange(sent)
    d = exchange(to_groups(d_out[0]))
    e, ep, o, li = forward(meta, pack)
    moved_out = shifted(to_tokens(exchange(o)), 1)
    dq, dkv = backward(meta, pack, d, e, ep, o, li)
    moved_q = shifted(to_tokens(exchange(dq)), -1)
    parts = exchange(dkv).reshape(SPLIT, -1, 2, TOK, HD).astype(F32).sum(axis=0).astype(BF16)
    sums = jnp.transpose(parts, (1, 2, 0, 3)).reshape(2, TOK, -1)
    moved_kv = shifted(sums, -1)
    return (moved_out[None], moved_q[None], moved_kv[0][None], moved_kv[1][None])


def solution(mesh):
    spec = P("section", ("blk", "uly"), None)
    return jax.shard_map(
        shards,
        mesh=mesh,
        in_specs=(spec,) * 6 + (P(),),
        out_specs=(spec,) * 4,
        check_vma=False,
    )
```

time: 490 us -> 280 us (0.57); the launches traced: 481 us -> 278 us
  waiting for transfers between devices: 248 us -> 69.8 us
  Pallas kernels: 0 us -> 87.8 us
  matrix products: 67 us -> 0 us
  starting transfers between devices: 49.1 us -> 25.3 us
  other arithmetic: 15.6 us -> 1.01 us
  blocking collectives: 38 us -> 52.4 us
  between operations: 14.3 us -> 0.77 us
  local copies, waits for them, and re-layouts: 48 us -> 40.9 us
    reduce_scatter x1 -> x0, waiting for transfers between devices: 178 us -> none  [shards(): lax.psum_scatter(grads.astype(jnp.bfloat16), 'blk', scatter_dimension=0,...]
    pallas_call x0 -> x2, Pallas kernels: none -> 87.8 us  [the longest x1 47 us: forward(): pl.pallas_call(forward_kernel, grid_spec=pltpu.PrefetchScalarGridSpec(num...]
    dot_general x17 -> x0, matrix products: 67 us -> none  [the longest x3 21.6 us: weight_step(): jnp.einsum('kgrn,nkd->kgrd', prob.astype(jnp.bfloat16), block_values, pre...]
    all_to_all x1 -> x2, blocking collectives: 15.7 us -> 52.4 us  [exchange(): lax.all_to_all(x, ('blk', 'uly'), split_axis=0, concat_axis=0, tiled=True)]
    all_gather x2 -> x0, blocking collectives: 22.3 us -> none  [the longest x1 17 us: shards(): lax.all_gather(pv_part, 'blk', axis=0, tiled=True)]
    ppermute x4 -> x3, waiting for transfers between devices: 0.01 us -> 19.7 us  [shifted(): lax.ppermute(block, 'section', [((i - distance) % count, i) for i in rang...]
    all_to_all x9 -> x3, waiting for transfers between devices: 69.7 us -> 50.1 us  [exchange(): lax.all_to_all(x, ('blk', 'uly'), split_axis=0, concat_axis=0, tiled=True)]
    all_to_all x9 -> x3, starting transfers between devices: 39.3 us -> 19.8 us  [exchange(): lax.all_to_all(x, ('blk', 'uly'), split_axis=0, concat_axis=0, tiled=True)]
  transfers between devices with their start and end apart: 16 -> 6, of which waited for: 9 -> 3; matrix products, arithmetic and copies ran while one was open for 13% -> 9% of each run, Pallas kernels for 0% -> 17%
where the time goes in v1:
time: 280 us; the launch traced here: 278 us
  Pallas kernels  87.8 us (31%)
  waiting for transfers between devices  69.8 us (25%)
  blocking collectives  52.4 us (19%)
  local copies, waits for them, and re-layouts  40.9 us (15%)
  starting transfers between devices  25.3 us (9%)
    all_to_all x2, blocking collectives, exchange(): lax.all_to_all(x, ('blk', 'uly'), split_axis=0, concat_axis=0, tiled=True)  52.4 us
    all_to_all x3, waiting for transfers between devices, exchange(): lax.all_to_all(x, ('blk', 'uly'), split_axis=0, concat_axis=0, tiled=True)  50.1 us
    pallas_call x1, Pallas kernels, forward(): pl.pallas_call(forward_kernel, grid_spec=pltpu.PrefetchScalarGridSpec(num...  47 us
    pallas_call x1, Pallas kernels, backward(): pl.pallas_call(backward_kernel, grid_spec=pltpu.PrefetchScalarGridSpec(nu...  40.8 us
    all_to_all x3, starting transfers between devices, exchange(): lax.all_to_all(x, ('blk', 'uly'), split_axis=0, concat_axis=0, tiled=True)  19.8 us
    ppermute x3, waiting for transfers between devices, shifted(): lax.ppermute(block, 'section', [((i - distance) % count, i) for i in rang...  19.7 us
    unnamed x26, local copies, waits for them, and re-layouts  13.1 us
    reshape x2, local copies, waits for them, and re-layouts, to_tokens(): return jnp.transpose(x, (0, 3, 1, 2, 4)).reshape(TOK, -1)  8.07 us
  transfers between devices with their start and end apart: 6, of which 3 were waited for; matrix products, arithmetic and copies ran while one was open for 9% of the time, Pallas kernels for 17%

profile of v1, /device:TPU:0, one launch (start us, length us, event | category | flops | bytes accessed | tf_op | source)
XLA Modules:
  0.0 278.1 jit_solution(16154093372594857666)
XLA Ops:
  0.6 0.0 copy-start.2
  0.6 1.1 copy.40
  1.7 0.7 copy.32
  2.5 1.0 copy.41
  3.5 0.7 copy.33
  4.2 0.0 copy-done.2
  4.2 1.6 reshape_squeeze.18
  5.8 1.5 copy.31
  7.4 0.0 copy-start.4
  7.4 1.3 constant_dynamic-update-slice_fusion.4
  8.7 0.2 broadcast_in_dim.15
  8.9 1.2 constant_dynamic-update-slice_fusion.3
  10.1 0.2 broadcast_in_dim.16
  10.4 1.2 constant_dynamic-update-slice_fusion.2
  11.6 0.6 constant_dynamic-update-slice_fusion.1
  12.2 0.0 copy-done.6
  12.2 0.6 constant_dynamic-update-slice_fusion
  12.9 8.4 %all-to-all-start = ((bf16[32,432,128]{2,1,0:T(8,128)(2,1)}), bf16[32,432,128]{2,1,0:T(8,128)(2,1)S(1)}, u32[]{:S(2)}, u32[]{:S(2)}) async-start(bf16[32,432,128]{2,1,0:T(8,128)(2,1)} %constant_dynamic-update-slice_fusion), calls=%async_computation | async-start | bytes 7077888 | tf_op jit(solution)/shard_map/all_to_all | solution.py:315
  21.3 4.2 %reshape_squeeze.23 = bf16[4,32,8,5,128]{4,3,2,1,0:T(8,128)(2,1)} reshape(bf16[1,128,5120]{2,1,0:T(8,128)(2,1)} %param.14) | data formatting | bytes 2621440 | tf_op jit(solution)/shard_map/reshape;squeeze | solution.py:299
  25.5 4.2 %copy.35 = bf16[4,8,5,32,128]{4,3,2,1,0:T(8,128)(2,1)} copy(bf16[4,8,5,32,128]{4,2,1,3,0:T(8,128)(2,1)} %bitcast.42) | data formatting | bytes 2621440 | tf_op jit(solution)/shard_map/transpose | solution.py:300
  29.7 37.7 %all-to-all-done.pack = bf16[32,432,128]{2,1,0:T(8,128)(2,1)S(1)} async-done(((bf16[32,432,128]{2,1,0:T(8,128)(2,1)}), bf16[32,432,128]{2,1,0:T(8,128)(2,1)S(1)}, u32[]{:S(2)}, u32[]{:S(2)}) %all-to-all-start) | async-done | bytes 3538976 | tf_op jit(solution)/shard_map/all_to_all | solution.py:315
  67.4 7.1 %all-to-all-start.2 = ((bf16[32,160,128]{2,1,0:T(8,128)(2,1)}), bf16[32,160,128]{2,1,0:T(8,128)(2,1)}, u32[]{:S(2)}, u32[]{:S(2)}) async-start(bf16[32,160,128]{2,1,0:T(8,128)(2,1)} %bitcast.43), calls=%async_computation.2 | async-start | bytes 2621440 | tf_op jit(solution)/shard_map/all_to_all | solution.py:315
  74.5 0.0 copy-done.7
  74.5 0.6 pad_add_fusion.meta
  75.1 0.0 copy-done
  75.1 47.0 %forward.1 = (bf16[20,1280,512]{2,1,0:T(8,128)(2,1)}, bf16[4,1280,256]{2,1,0:T(8,128)(2,1)}, bf16[32,160,128]{2,1,0:T(8,128)(2,1)}, f32[5120,128]{1,0:T(8,128)}) custom-call(s32[20]{0:T(128)} %constant.12.clone.row_of, s32[20]{0:T(128)} %constant.13.clone.key_of, s32[5]{0:T(128)} %pad_add_fusion.meta, bf16[32,432,128]{2,1,0:T(8,128)(2,1)} %copy-done), custom_call_target="tpu_custom_call" | custom-call | tf_op jit(solution)/shard_map/forward/pallas_call | solution.py:171
  122.2 0.0 all-to-all-done.2.d_in
  122.2 40.8 %backward.1 = (bf16[32,160,128]{2,1,0:T(8,128)(2,1)}, bf16[32,256,128]{2,1,0:T(8,128)(2,1)}) custom-call(s32[20]{0:T(128)} %constant.12.clone.row_of, s32[20]{0:T(128)} %constant.13.clone.key_of, s32[5]{0:T(128)} %pad_add_fusion.meta, bf16[32,432,128]{2,1,0:T(8,128)(2,1)} %copy-done, bf16[32,160,128]{2,1,0:T(8,128)(2,1)} %all-to-all-done.2.d_in, ...), custom_call_target="tpu_custom_call" | custom-call | tf_op jit(solution)/shard_map/backward/pallas_call | solution.py:265
  162.9 28.0 %all_to_all.25 = bf16[32,160,128]{2,1,0:T(8,128)(2,1)S(1)} all-to-all(bf16[32,160,128]{2,1,0:T(8,128)(2,1)} %get-tuple-element.14), channel_id=1, replica_groups=mesh['section'=4,'blk'=4,'uly'=8] {'blk','uly'}, dimensions={0} | all-to-all | bytes 2621440 | tf_op jit(solution)/shard_map/all_to_all | solution.py:315
  191.0 24.4 %all_to_all.26 = bf16[32,160,128]{2,1,0:T(8,128)(2,1)} all-to-all(bf16[32,160,128]{2,1,0:T(8,128)(2,1)S(1)} %copy-done.1), channel_id=1, replica_groups=mesh['section'=4,'blk'=4,'uly'=8] {'blk','uly'}, dimensions={0} | all-to-all | bytes 2621440 | tf_op jit(solution)/shard_map/all_to_all | solution.py:315
  215.4 4.2 %all-to-all-start.4 = ((bf16[32,256,128]{2,1,0:T(8,128)(2,1)}), bf16[32,256,128]{2,1,0:T(8,128)(2,1)S(1)}, u32[]{:S(2)}, u32[]{:S(2)}) async-start(bf16[32,256,128]{2,1,0:T(8,128)(2,1)} %get-tuple-element.15), calls=%async_computation.4 | async-start | bytes 4194304 | tf_op jit(solution)/shard_map/all_to_all | solution.py:315
  219.6 3.3 %copy.45 = bf16[4,8,5,32,128]{4,2,1,3,0:T(8,128)(2,1)} copy(bf16[4,8,5,32,128]{4,3,2,1,0:T(8,128)(2,1)} %bitcast.45) | data formatting | bytes 2621440 | tf_op jit(solution)/shard_map/reshape | solution.py:304
  223.0 2.0 copy.44
  225.0 4.0 %reshape.57 = bf16[128,5120]{1,0:T(8,128)(2,1)} reshape(bf16[4,32,8,5,128]{4,3,2,1,0:T(8,128)(2,1)} %bitcast.40) | data formatting | bytes 2621440 | tf_op jit(solution)/shard_map/reshape | solution.py:305
  229.0 2.7 collective-permute-start.1
  231.7 4.0 %reshape.54 = bf16[128,5120]{1,0:T(8,128)(2,1)} reshape(bf16[4,32,8,5,128]{4,3,2,1,0:T(8,128)(2,1)} %bitcast.39) | data formatting | bytes 2621440 | tf_op jit(solution)/shard_map/reshape | solution.py:305
  235.8 0.0 collective-permute-start
  235.8 12.3 %all-to-all-done.4 = bf16[32,256,128]{2,1,0:T(8,128)(2,1)S(1)} async-done(((bf16[32,256,128]{2,1,0:T(8,128)(2,1)}), bf16[32,256,128]{2,1,0:T(8,128)(2,1)S(1)}, u32[]{:S(2)}, u32[]{:S(2)}) %all-to-all-start.4) | async-done | bytes 2097184 | tf_op jit(solution)/shard_map/all_to_all | solution.py:315
  248.1 0.4 reduce_sum.12
  248.6 0.3 copy.37
  248.8 2.8 %collective-permute-start.2 = (bf16[2,128,1024]{1,2,0:T(8,128)(2,1)S(1)}, bf16[2,128,1024]{1,2,0:T(8,128)(2,1)S(1)}, u32[]{:S(2)}, u32[]{:S(2)}) collective-permute-start(bf16[2,128,1024]{1,2,0:T(8,128)(2,1)S(1)} %bitcast.52), channel_id=1, source_target_pairs={{32,0},{64,32},{96,64},{0,96},{33,1},{65,33},{97,65},{1,97},{34,2}... | collective-permute-start | bytes 1572872 | tf_op jit(solution)/shard_map/ppermute | solution.py:320
  251.7 19.7 %collective-permute-done.2 = bf16[2,128,1024]{1,2,0:T(8,128)(2,1)S(1)} collective-permute-done((bf16[2,128,1024]{1,2,0:T(8,128)(2,1)S(1)}, bf16[2,128,1024]{1,2,0:T(8,128)(2,1)S(1)}, u32[]{:S(2)}, u32[]{:S(2)}) %collective-permute-start.2) | collective-permute-done | bytes 524320 | tf_op jit(solution)/shard_map/ppermute | solution.py:320
  271.4 0.9 copy.39
  272.3 0.8 copy.38
  273.1 0.0 collective-permute-done.1
  273.1 0.0 collective-permute-done
  273.1 2.5 copy.52
  275.6 2.5 copy.53
  (13 shorter events, 0.1 us)
Async XLA Ops:
  0.6 3.6 %copy-start.2 = (bf16[1,128,5120]{2,1,0:T(8,128)(2,1)S(1)}, bf16[1,128,5120]{2,1,0:T(8,128)(2,1)}, u32[]{:S(2)}) copy-start(bf16[1,128,5120]{2,1,0:T(8,128)(2,1)} %param.9) | copy-start | bytes 3932164
  7.4 1.3 copy-start.4
  8.7 1.4 copy-start.3
  10.1 1.4 copy-start.5
  10.1 2.1 copy-start.6
  12.9 54.5 %all-to-all-start = ((bf16[32,432,128]{2,1,0:T(8,128)(2,1)}), bf16[32,432,128]{2,1,0:T(8,128)(2,1)S(1)}, u32[]{:S(2)}, u32[]{:S(2)}) async-start(bf16[32,432,128]{2,1,0:T(8,128)(2,1)} %constant_dynamic-update-slice_fusion), calls=%async_computation | async-start | bytes 7077888 | tf_op jit(solution)/shard_map/all_to_all | solution.py:315
  29.7 44.9 %copy-start.7 = (s32[4]{0:T(128)S(1)}, s32[4]{0:T(128)}, u32[]{:S(2)}) copy-start(s32[4]{0:T(128)} %param.15) | copy-start | bytes 52
  67.4 7.8 %copy-start = (bf16[32,432,128]{2,1,0:T(8,128)(2,1)}, bf16[32,432,128]{2,1,0:T(8,128)(2,1)S(1)}, u32[]{:S(2)}) copy-start(bf16[32,432,128]{2,1,0:T(8,128)(2,1)S(1)} %all-to-all-done.pack) | copy-start | bytes 10616836
  67.4 54.8 %all-to-all-start.2 = ((bf16[32,160,128]{2,1,0:T(8,128)(2,1)}), bf16[32,160,128]{2,1,0:T(8,128)(2,1)}, u32[]{:S(2)}, u32[]{:S(2)}) async-start(bf16[32,160,128]{2,1,0:T(8,128)(2,1)} %bitcast.43), calls=%async_computation.2 | async-start | bytes 2621440 | tf_op jit(solution)/shard_map/all_to_all | solution.py:315
  162.9 28.0 %copy-start.1 = (bf16[32,160,128]{2,1,0:T(8,128)(2,1)S(1)}, bf16[32,160,128]{2,1,0:T(8,128)(2,1)}, u32[]{:S(2)}) copy-start(bf16[32,160,128]{2,1,0:T(8,128)(2,1)} %get-tuple-element.10.o_in) | copy-start | bytes 3932164
  215.4 32.7 %all-to-all-start.4 = ((bf16[32,256,128]{2,1,0:T(8,128)(2,1)}), bf16[32,256,128]{2,1,0:T(8,128)(2,1)S(1)}, u32[]{:S(2)}, u32[]{:S(2)}) async-start(bf16[32,256,128]{2,1,0:T(8,128)(2,1)} %get-tuple-element.15), calls=%async_computation.4 | async-start | bytes 4194304 | tf_op jit(solution)/shard_map/all_to_all | solution.py:315
  229.0 44.1 %collective-permute-start.1 = (bf16[128,5120]{1,0:T(8,128)(2,1)}, bf16[128,5120]{1,0:T(8,128)(2,1)}, u32[]{:S(2)}, u32[]{:S(2)}) collective-permute-start(bf16[128,5120]{1,0:T(8,128)(2,1)} %reshape.57), channel_id=1, source_target_pairs={{32,0},{64,32},{96,64},{0,96},{33,1},{65,33},{97,65},{1,97},{34,2}... | collective-permute-start | bytes 3932168 | tf_op jit(solution)/shard_map/ppermute | solution.py:320
  235.8 37.4 %collective-permute-start = (bf16[128,5120]{1,0:T(8,128)(2,1)}, bf16[128,5120]{1,0:T(8,128)(2,1)}, u32[]{:S(2)}, u32[]{:S(2)}) collective-permute-start(bf16[128,5120]{1,0:T(8,128)(2,1)} %reshape.54), channel_id=1, source_target_pairs={{96,0},{0,32},{32,64},{64,96},{97,1},{1,33},{33,65},{65,97},{98,2}... | collective-permute-start | bytes 3932168 | tf_op jit(solution)/shard_map/ppermute | solution.py:320
  248.8 22.5 %collective-permute-start.2 = (bf16[2,128,1024]{1,2,0:T(8,128)(2,1)S(1)}, bf16[2,128,1024]{1,2,0:T(8,128)(2,1)S(1)}, u32[]{:S(2)}, u32[]{:S(2)}) collective-permute-start(bf16[2,128,1024]{1,2,0:T(8,128)(2,1)S(1)} %bitcast.52), channel_id=1, source_target_pairs={{32,0},{64,32},{96,64},{0,96},{33,1},{65,33},{97,65},{1,97},{34,2}... | collective-permute-start | bytes 1572872 | tf_op jit(solution)/shard_map/ppermute | solution.py:320

commit v2 on v1

v2 whole, which is shorter than its diff:
```python
import math

import jax
import jax.numpy as jnp
import numpy as np
from jax import lax
from jax.experimental import pallas as pl
from jax.experimental.pallas import tpu as pltpu
from jax.sharding import PartitionSpec as P

HD = 128
GROUP = 5
CHUNKS = 32
TOK = 128
SPLIT = 4
SUB = TOK // SPLIT
QR = GROUP * SUB
PRE = 8
K0, V0, P0 = QR, QR + TOK, QR + 2 * TOK
PACK = P0 + 2 * PRE
RC = 8
KC = 4
M = RC * QR
N = KC * TOK
HALF = M // 2
N_RB = CHUNKS // RC
PTOT = CHUNKS * PRE
SCALE = 1.0 / math.sqrt(HD)
SAFE = 60.0
NEG = -1e30
F32 = jnp.float32
BF16 = jnp.bfloat16
VMEM = 40 * 2**20

ROW_OF = np.array([r for r in reversed(range(N_RB)) for _ in range(2 * r + 2)], np.int32)
KEY_OF = np.array([k for r in reversed(range(N_RB)) for k in range(2 * r + 2)], np.int32)
STEPS = len(ROW_OF)


def COST(products):
    entries = (STEPS + N_RB) * M * N
    return pl.CostEstimate(
        flops=products * 2 * entries * HD, transcendentals=entries, bytes_accessed=products * entries
    )


def dot(a, b, ca, cb):
    return lax.dot_general(a, b, (((ca,), (cb,)), ((), ())), preferred_element_type=F32)


def wide(x, width):
    return jnp.concatenate([x] * (width // x.shape[1]), axis=1)


def row_norm(x):
    return jnp.max(dot(x * x, jnp.ones((HD, HD), BF16), 1, 0))


def row_pos(chunks, width, part):
    shape = (chunks, GROUP, SUB, width)
    pos = lax.broadcasted_iota(jnp.int32, shape, 0) * TOK + lax.broadcasted_iota(jnp.int32, shape, 2)
    return pos.reshape(chunks * QR, width) + part * SUB


def key_pos(rows, width):
    return lax.broadcasted_iota(jnp.int32, (rows, width), 1)


def prefix_live(fill_ref, rows):
    pos = key_pos(rows, PTOT)
    live = pos < 0
    block = PTOT // SPLIT
    for b in range(SPLIT):
        live = live | ((pos >= b * block) & (pos < b * block + fill_ref[b]))
    return live


def prefix_rows(pack_ref, which):
    both = pack_ref[:, P0:PACK, :].astype(F32)
    return both[:, which * PRE : (which + 1) * PRE].reshape(PTOT, HD).astype(BF16)


def forward_kernel(row_of, key_of, meta, pack, e_out, o_out, li_out, acc, shift, pk, pv, knorm):
    t = pl.program_id(0)
    rb, kb = row_of[t], key_of[t]
    part = meta[SPLIT]

    @pl.when(t == 0)
    def _():
        pk[...] = prefix_rows(pack, 0)
        pv[...] = prefix_rows(pack, 1)
        knorm[0] = jnp.maximum(row_norm(pk[...]), row_norm(pack[:, K0:V0, :].reshape(CHUNKS * TOK, HD)))

    def queries():
        return pack[pl.ds(rb * RC, RC), 0:QR, :].reshape(M, HD)

    @pl.when(kb == 0)
    def _():
        acc[...] = jnp.zeros_like(acc)
        shift[...] = jnp.zeros_like(shift)
        q = queries()
        qnorm = row_norm(q)

        @pl.when(jnp.logical_not(qnorm * knorm[0] * (SCALE * SCALE) <= SAFE * SAFE))
        def _():
            live = prefix_live(meta, M)
            s = jnp.where(live, dot(q, pk[...], 1, 1) * SCALE, NEG)
            shift[...] = jnp.broadcast_to(jnp.max(s, axis=1, keepdims=True), shift.shape)

            def step(k, carry):
                keys = pack[pl.ds(k * KC, KC), K0:V0, :].reshape(N, HD)
                pos = row_pos(RC, N, part) + rb * (RC * TOK)
                s = jnp.where(key_pos(M, N) + k * N <= pos, dot(q, keys, 1, 1) * SCALE, NEG)
                top = jnp.broadcast_to(jnp.max(s, axis=1, keepdims=True), shift.shape)
                shift[...] = jnp.maximum(shift[...], top)
                return carry

            lax.fori_loop(0, 2 * rb + 2, step, 0)

    def tile(first, keys, values, live=None, at=None):
        width = keys.shape[0]
        row, col = at or (first, 0)
        q = pack[pl.ds(rb * RC + first // QR, RC // 2), 0:QR, :].reshape(HALF, HD)
        e = jnp.exp(dot(q, keys, 1, 1) * SCALE - wide(shift[first : first + HALF, :], width))
        if live is not None:
            e = jnp.where(live, e, 0.0)
        e = e.astype(BF16)
        e_out[0, row : row + HALF, col : col + width] = e
        both = jnp.concatenate([values, jnp.ones_like(values)], axis=1)
        acc[first : first + HALF, :] += dot(e, both, 1, 0)

    keys = pack[pl.ds(kb * KC, KC), K0:V0, :].reshape(N, HD)
    values = pack[pl.ds(kb * KC, KC), V0:P0, :].reshape(N, HD)
    causal = lambda: key_pos(HALF, N) <= row_pos(RC // 2, N, part)

    @pl.when(kb < 2 * rb)
    def _():
        tile(0, keys, values)

    @pl.when(kb <= 2 * rb)
    def _():
        tile(HALF, keys, values)

    @pl.when(kb == 2 * rb)
    def _():
        tile(0, keys, values, causal())

    @pl.when(kb == 2 * rb + 1)
    def _():
        tile(HALF, keys, values, causal())
        live = prefix_live(meta, HALF)
        for half in range(2):
            tile(half * HALF, pk[...], pv[...], live, (0, half * PTOT))
        inverse = 1.0 / acc[:, HD:]
        li_out[...] = inverse
        o_out[...] = (acc[:, :HD] * inverse).astype(BF16).reshape(RC, QR, HD)


def forward(meta, pack):
    return pl.pallas_call(
        forward_kernel,
        grid_spec=pltpu.PrefetchScalarGridSpec(
            num_scalar_prefetch=3,
            grid=(STEPS,),
            in_specs=[pl.BlockSpec(memory_space=pltpu.VMEM)],
            out_specs=[
                pl.BlockSpec((1, M, N), lambda t, r, k, m: (t, 0, 0)),
                pl.BlockSpec((RC, QR, HD), lambda t, r, k, m: (r[t], 0, 0)),
                pl.BlockSpec((M, HD), lambda t, r, k, m: (r[t], 0)),
            ],
            scratch_shapes=[
                pltpu.VMEM((M, 2 * HD), F32),
                pltpu.VMEM((M, HD), F32),
                pltpu.VMEM((PTOT, HD), BF16),
                pltpu.VMEM((PTOT, HD), BF16),
                pltpu.SMEM((1,), F32),
            ],
        ),
        out_shape=[
            jax.ShapeDtypeStruct((STEPS, M, N), BF16),
            jax.ShapeDtypeStruct((CHUNKS, QR, HD), BF16),
            jax.ShapeDtypeStruct((N_RB * M, HD), F32),
        ],
        compiler_params=pltpu.CompilerParams(vmem_limit_bytes=VMEM),
        cost_estimate=COST(2),
        name="forward",
    )(jnp.asarray(ROW_OF), jnp.asarray(KEY_OF), meta, pack)


def backward_kernel(row_of, key_of, meta, pack, d_in, e_in, o_in, li_in, dq_out, dkv_out, dq, dk, dv, dn, delta, pk, pv):
    t = pl.program_id(0)
    rb, kb = row_of[t], key_of[t]
    part = meta[SPLIT]

    @pl.when(t == 0)
    def _():
        pk[...] = prefix_rows(pack, 0)
        pv[...] = prefix_rows(pack, 1)

    @pl.when(kb == 0)
    def _():
        dq[...] = jnp.zeros_like(dq)
        d = (d_in[...].reshape(M, HD).astype(F32) * (li_in[...] * SCALE)).astype(BF16)
        dn[...] = d
        total = jnp.sum(d.astype(F32) * o_in[...].reshape(M, HD).astype(F32), axis=1, keepdims=True)
        delta[...] = jnp.broadcast_to(total, delta.shape)

    here = pl.ds(kb * N, N)

    @pl.when(rb == N_RB - 1)
    def _():
        dk[here, :] = jnp.zeros((N, HD), F32)
        dv[here, :] = jnp.zeros((N, HD), F32)

    def tile(first, keys, values, at=None):
        width = keys.shape[0]
        row, col = at or (first, 0)
        d = dn[first : first + HALF, :]
        e = e_in[0, row : row + HALF, col : col + width]
        dp = dot(d, values, 1, 1) - wide(delta[first : first + HALF, :], width)
        ds = (e.astype(F32) * dp).astype(BF16)
        dq[first : first + HALF, :] += dot(ds, keys, 1, 0)
        if at is None:
            q = pack[pl.ds(rb * RC + first // QR, RC // 2), 0:QR, :].reshape(HALF, HD)
            dv[here, :] += dot(e, d, 0, 0)
            dk[here, :] += dot(ds, q, 0, 0)

    keys = pack[pl.ds(kb * KC, KC), K0:V0, :].reshape(N, HD)
    values = pack[pl.ds(kb * KC, KC), V0:P0, :].reshape(N, HD)

    @pl.when(kb <= 2 * rb)
    def _():
        tile(0, keys, values)

    tile(HALF, keys, values)

    @pl.when(kb == 2 * rb + 1)
    def _():
        for half in range(2):
            tile(half * HALF, pk[...], pv[...], (0, half * PTOT))
        dq_out[...] = dq[...].astype(BF16).reshape(RC, QR, HD)

    @pl.when(kb >= 2 * rb)
    def _():
        dkv_out[:, 0:TOK, :] = dk[here, :].astype(BF16).reshape(KC, TOK, HD)
        dkv_out[:, TOK:, :] = (dv[here, :] * (1.0 / SCALE)).astype(BF16).reshape(KC, TOK, HD)


def backward(meta, pack, d, e, o, li):
    by_rows = lambda *shape: pl.BlockSpec(shape, lambda t, r, k, m: (r[t],) + (0,) * (len(shape) - 1))
    return pl.pallas_call(
        backward_kernel,
        grid_spec=pltpu.PrefetchScalarGridSpec(
            num_scalar_prefetch=3,
            grid=(STEPS,),
            in_specs=[
                pl.BlockSpec(memory_space=pltpu.VMEM),
                by_rows(RC, QR, HD),
                pl.BlockSpec((1, M, N), lambda t, r, k, m: (t, 0, 0)),
                by_rows(RC, QR, HD),
                by_rows(M, HD),
            ],
            out_specs=[
                by_rows(RC, QR, HD),
                pl.BlockSpec((KC, 2 * TOK, HD), lambda t, r, k, m: (jnp.maximum(k[t], 2 * r[t]), 0, 0)),
            ],
            scratch_shapes=[
                pltpu.VMEM((M, HD), F32),
                pltpu.VMEM((CHUNKS * TOK, HD), F32),
                pltpu.VMEM((CHUNKS * TOK, HD), F32),
                pltpu.VMEM((M, HD), BF16),
                pltpu.VMEM((M, HD), F32),
                pltpu.VMEM((PTOT, HD), BF16),
                pltpu.VMEM((PTOT, HD), BF16),
            ],
        ),
        out_shape=[
            jax.ShapeDtypeStruct((CHUNKS, QR, HD), BF16),
            jax.ShapeDtypeStruct((CHUNKS, 2 * TOK, HD), BF16),
        ],
        compiler_params=pltpu.CompilerParams(vmem_limit_bytes=VMEM),
        cost_estimate=COST(4),
        name="backward",
    )(jnp.asarray(ROW_OF), jnp.asarray(KEY_OF), meta, pack, d, e, o, li)


GROUPS = CHUNKS // SPLIT
AT_ONCE = 4


def cols(rows, width):
    return pl.BlockSpec((1, rows, AT_ONCE * width), lambda g: (0, 0, g))


def parts_of(rows):
    return pl.BlockSpec((SPLIT, AT_ONCE, rows, HD), lambda g: (0, g, 0, 0))


def each_head():
    for g in range(AT_ONCE):
        for h in range(GROUP):
            at = (g * GROUP + h) * HD
            yield g, slice(h * SUB, (h + 1) * SUB), slice(at, at + HD)


def gather_kernel(*refs):
    queries, rest, out = refs[0], refs[1:-1], refs[-1]
    for j in range(SPLIT):
        for g, rows, at in each_head():
            out[j, g, rows, :] = queries[0, j * SUB : (j + 1) * SUB, at]
    if rest:
        keys, values, pre_keys, pre_values = rest
        for g in range(AT_ONCE):
            at = slice(g * HD, (g + 1) * HD)
            prefix = jnp.concatenate([pre_keys[0, :, at].astype(F32), pre_values[0, :, at].astype(F32)], axis=0)
            prefix = prefix.astype(BF16)
            for j in range(SPLIT):
                out[j, g, K0:V0, :] = keys[0, :, at]
                out[j, g, V0:P0, :] = values[0, :, at]
                out[j, g, P0:PACK, :] = prefix


def gather(queries, *rest):
    rows = PACK if rest else QR
    packed = pl.pallas_call(
        gather_kernel,
        grid=(GROUPS // AT_ONCE,),
        in_specs=[cols(x.shape[1], x.shape[2] // GROUPS) for x in (queries,) + rest],
        out_specs=parts_of(rows),
        out_shape=jax.ShapeDtypeStruct((SPLIT, GROUPS, rows, HD), BF16),
        compiler_params=pltpu.CompilerParams(vmem_limit_bytes=VMEM),
        name="gather",
    )(queries, *rest)
    return packed.reshape(CHUNKS, rows, HD)


def spread_kernel(packed, out):
    for j in range(SPLIT):
        for g, rows, at in each_head():
            out[0, j * SUB : (j + 1) * SUB, at] = packed[j, g, rows, :]


def spread(packed):
    return pl.pallas_call(
        spread_kernel,
        grid=(GROUPS // AT_ONCE,),
        in_specs=[parts_of(QR)],
        out_specs=cols(TOK, GROUP * HD),
        out_shape=jax.ShapeDtypeStruct((1, TOK, GROUPS * GROUP * HD), BF16),
        compiler_params=pltpu.CompilerParams(vmem_limit_bytes=VMEM),
        name="spread",
    )(packed.reshape(SPLIT, GROUPS, QR, HD))


def sum_kernel(parts, keys, values):
    for g in range(AT_ONCE):
        total = parts[0, g].astype(F32)
        for j in range(1, SPLIT):
            total += parts[j, g].astype(F32)
        keys[0, :, g * HD : (g + 1) * HD] = total[:TOK].astype(BF16)
        values[0, :, g * HD : (g + 1) * HD] = total[TOK:].astype(BF16)


def sum_parts(parts):
    shape = jax.ShapeDtypeStruct((1, TOK, GROUPS * HD), BF16)
    return pl.pallas_call(
        sum_kernel,
        grid=(GROUPS // AT_ONCE,),
        in_specs=[parts_of(2 * TOK)],
        out_specs=[cols(TOK, HD), cols(TOK, HD)],
        out_shape=[shape, shape],
        compiler_params=pltpu.CompilerParams(vmem_limit_bytes=VMEM),
        name="sum_parts",
    )(parts.reshape(SPLIT, GROUPS, 2 * TOK, HD))


def exchange(x):
    return lax.all_to_all(x, ("blk", "uly"), split_axis=0, concat_axis=0, tiled=True)


def shifted(block, distance):
    count = lax.axis_size("section")
    return lax.ppermute(block, "section", [((i - distance) % count, i) for i in range(count)])


def shards(queries, keys, values, pre_keys, pre_values, d_out, prefix_fill):
    part = lax.axis_index("blk").astype(jnp.int32)
    meta = jnp.concatenate([prefix_fill, part[None]])
    pack = exchange(gather(queries, keys, values, pre_keys, pre_values))
    d = exchange(gather(d_out))
    pack = pltpu.with_memory_space_constraint(pack, pltpu.VMEM)
    e, o, li = forward(meta, pack)
    next_input = shifted(spread(exchange(o)), 1)
    dq, dkv = backward(meta, pack, d, e, o, li)
    query_grad = spread(exchange(shifted(dq, -1)))
    key_grad, value_grad = (shifted(x, -1) for x in sum_parts(exchange(dkv)))
    return (next_input, query_grad, key_grad, value_grad)


def solution(mesh):
    spec = P("section", ("blk", "uly"), None)
    return jax.shard_map(
        shards,
        mesh=mesh,
        in_specs=(spec,) * 6 + (P(),),
        out_specs=(spec,) * 4,
        check_vma=False,
    )
```

time: 280 us -> 243 us (0.87)
  blocking collectives: 52.4 us -> 0 us
  local copies, waits for them, and re-layouts: 40.9 us -> 20.4 us
  starting transfers between devices: 25.3 us -> 44.2 us
  waiting for transfers between devices: 69.8 us -> 87.3 us
    all_to_all x2 -> x0, blocking collectives: 52.4 us -> none  [exchange(): lax.all_to_all(x, ('blk', 'uly'), split_axis=0, concat_axis=0, tiled=True)]
    ppermute x3 -> x4, waiting for transfers between devices: 19.7 us -> 39.1 us  [shifted(): lax.ppermute(block, 'section', [((i - distance) % count, i) for i in rang...]
    all_to_all x3 -> x5, starting transfers between devices: 19.8 us -> 37.6 us  [exchange(): lax.all_to_all(x, ('blk', 'uly'), split_axis=0, concat_axis=0, tiled=True)]
    reshape x4 -> x0, local copies, waits for them, and re-layouts: 13.4 us -> none  [the longest x2 8.07 us: to_tokens(): return jnp.transpose(x, (0, 3, 1, 2, 4)).reshape(TOK, -1)]
    transpose x5 -> x0, local copies, waits for them, and re-layouts: 7.47 us -> none  [the longest x2 5.69 us: to_groups(): return jnp.transpose(x, (0, 2, 3, 1, 4)).reshape(CHUNKS, QR, HD)]
    unnamed x26 -> x37, local copies, waits for them, and re-layouts: 13.1 us -> 20.4 us
    pallas_call x0 -> x5, Pallas kernels: none -> 6.48 us  [the longest x2 3.43 us: gather(): pl.pallas_call(gather_kernel, grid=(GROUPS // AT_ONCE,), in_specs=[cols(x...]
    another operation x2 -> x0, local copies, waits for them, and re-layouts: 5.76 us -> none  [to_groups(): x = x.reshape(SPLIT, SUB, -1, GROUP, HD)]
  transfers between devices with their start and end apart: 6 -> 9, of which waited for: 3 -> 5; matrix products, arithmetic and copies ran while one was open for 9% -> 0% of each run, Pallas kernels for 17% -> 36%
where the time goes in v2:
time: 243 us; the launch traced here: 241 us
  Pallas kernels  88.2 us (36%)
  waiting for transfers between devices  87.3 us (36%)
  starting transfers between devices  44.2 us (18%)
  local copies, waits for them, and re-layouts  20.4 us (8%)
    all_to_all x5, waiting for transfers between devices, exchange(): lax.all_to_all(x, ('blk', 'uly'), split_axis=0, concat_axis=0, tiled=True)  48.2 us
    pallas_call x1, Pallas kernels, forward(): pl.pallas_call(forward_kernel, grid_spec=pltpu.PrefetchScalarGridSpec(num...  43 us
    ppermute x4, waiting for transfers between devices, shifted(): lax.ppermute(block, 'section', [((i - distance) % count, i) for i in rang...  39.1 us
    pallas_call x1, Pallas kernels, backward(): pl.pallas_call(backward_kernel, grid_spec=pltpu.PrefetchScalarGridSpec(nu...  38.6 us
    all_to_all x5, starting transfers between devices, exchange(): lax.all_to_all(x, ('blk', 'uly'), split_axis=0, concat_axis=0, tiled=True)  37.6 us
    unnamed x37, local copies, waits for them, and re-layouts  20.4 us
    ppermute x4, starting transfers between devices, shifted(): lax.ppermute(block, 'section', [((i - distance) % count, i) for i in rang...  6.67 us
  transfers between devices with their start and end apart: 9, of which 5 were waited for; matrix products, arithmetic and copies ran while one was open for 0% of the time, Pallas kernels for 36%

profile of v2, /device:TPU:0, one launch (start us, length us, event | category | flops | bytes accessed | tf_op | source)
XLA Modules:
  0.0 240.9 jit_solution(9270453372917466511)
XLA Ops:
  0.6 0.0 copy-start.6
  0.6 1.3 copy-done.6
  2.0 0.9 copy-done.7
  2.9 0.9 copy-done.8
  3.9 0.7 copy-done.9
  4.6 0.7 copy-done.10
  5.3 2.2 gather.2
  7.4 8.4 %all-to-all-start = ((bf16[32,432,128]{2,1,0:T(8,128)(2,1)}), bf16[32,432,128]{2,1,0:T(8,128)(2,1)S(1)}, u32[]{:S(2)}, u32[]{:S(2)}) async-start(bf16[32,432,128]{2,1,0:T(8,128)(2,1)} %bitcast.1), calls=%async_computation | async-start | bytes 7077888 | tf_op jit(solution)/shard_map/all_to_all | solution.py:378
  15.9 0.0 copy-start.3
  15.9 1.3 copy-done.3
  17.2 1.3 gather.3
  18.5 43.5 %all-to-all-done.pack = bf16[32,432,128]{2,1,0:T(8,128)(2,1)S(1)} async-done(((bf16[32,432,128]{2,1,0:T(8,128)(2,1)}), bf16[32,432,128]{2,1,0:T(8,128)(2,1)S(1)}, u32[]{:S(2)}, u32[]{:S(2)}) %all-to-all-start) | async-done | bytes 3538976 | tf_op jit(solution)/shard_map/all_to_all | solution.py:378
  61.9 7.1 %all-to-all-start.2 = ((bf16[32,160,128]{2,1,0:T(8,128)(2,1)}), bf16[32,160,128]{2,1,0:T(8,128)(2,1)}, u32[]{:S(2)}, u32[]{:S(2)}) async-start(bf16[32,160,128]{2,1,0:T(8,128)(2,1)} %bitcast.3), calls=%async_computation.2 | async-start | bytes 2621440 | tf_op jit(solution)/shard_map/all_to_all | solution.py:378
  69.1 0.0 copy-done.16
  69.1 0.1 pad_add_fusion.meta
  69.1 0.0 copy-done.12
  69.1 0.0 copy-done.13
  69.1 43.0 %forward.1 = (bf16[20,1280,512]{2,1,0:T(8,128)(2,1)}, bf16[32,160,128]{2,1,0:T(8,128)(2,1)S(1)}, f32[5120,128]{1,0:T(8,128)S(1)}) custom-call(s32[20]{0:T(128)S(1)} %copy-done.13, s32[20]{0:T(128)S(1)} %copy-done.12, s32[5]{0:T(128)S(1)} %pad_add_fusion.meta, bf16[32,432,128]{2,1,0:T(8,128)(2,1)S(1)} %all-to-all-done.pack), custom_call_target="tpu_custom_call" | custom-call | flops 8053063680 | bytes 31457280 | tf_op jit(solution)/shard_map/forward/pallas_call | solution.py:160
  112.2 1.9 copy-done
  114.0 1.1 copy-done.4
  115.1 1.5 copy-done.14
  116.6 0.0 all-to-all-done.2.d_in
  116.6 7.4 %all-to-all-start.1 = ((bf16[32,160,128]{2,1,0:T(8,128)(2,1)}), bf16[32,160,128]{2,1,0:T(8,128)(2,1)S(1)}, u32[]{:S(2)}, u32[]{:S(2)}) async-start(bf16[32,160,128]{2,1,0:T(8,128)(2,1)} %copy-done.4), calls=%async_computation.1 | async-start | bytes 2621440 | tf_op jit(solution)/shard_map/all_to_all | solution.py:378
  124.0 0.0 copy-done.5
  124.0 2.0 copy-done.1
  126.0 1.7 copy-done.15
  127.8 38.6 %backward.1 = (bf16[32,160,128]{2,1,0:T(8,128)(2,1)S(1)}, bf16[32,256,128]{2,1,0:T(8,128)(2,1)S(1)}) custom-call(s32[20]{0:T(128)S(1)} %copy-done.13, s32[20]{0:T(128)S(1)} %copy-done.12, s32[5]{0:T(128)S(1)} %pad_add_fusion.meta, bf16[32,432,128]{2,1,0:T(8,128)(2,1)S(1)} %copy-done.1, bf16[32,160,128]{2,1,0:T(8,128)(2,1)} %all-to-all-done.2.d_in, ...), custom_call_target="tpu_custom_call" | custom-call | flops 16106127360 | bytes 62914560 | tf_op jit(solution)/shard_map/backward/pallas_call | solution.py:251
  166.4 1.3 copy-done.2
  167.8 1.1 copy-done.11
  168.9 0.0 all-to-all-done.1
  168.9 7.4 %all-to-all-start.4 = ((bf16[32,256,128]{2,1,0:T(8,128)(2,1)}), bf16[32,256,128]{2,1,0:T(8,128)(2,1)S(1)}, u32[]{:S(2)}, u32[]{:S(2)}) async-start(bf16[32,256,128]{2,1,0:T(8,128)(2,1)} %copy-done.2), calls=%async_computation.4 | async-start | bytes 4194304 | tf_op jit(solution)/shard_map/all_to_all | solution.py:378
  176.3 2.8 %collective-permute-start.1 = (bf16[32,160,128]{2,1,0:T(8,128)(2,1)}, bf16[32,160,128]{2,1,0:T(8,128)(2,1)}, u32[]{:S(2)}, u32[]{:S(2)}) collective-permute-start(bf16[32,160,128]{2,1,0:T(8,128)(2,1)} %copy-done.11), channel_id=1, source_target_pairs={{32,0},{64,32},{96,64},{0,96},{33,1},{65,33},{97,65},{1,97},{34,2}... | collective-permute-start | bytes 3932168 | tf_op jit(solution)/shard_map/ppermute | solution.py:383
  179.1 1.3 spread.2
  180.4 0.0 collective-permute-start
  180.4 27.5 %collective-permute-done.1 = bf16[32,160,128]{2,1,0:T(8,128)(2,1)} collective-permute-done((bf16[32,160,128]{2,1,0:T(8,128)(2,1)}, bf16[32,160,128]{2,1,0:T(8,128)(2,1)}, u32[]{:S(2)}, u32[]{:S(2)}) %collective-permute-start.1) | collective-permute-done | bytes 1310752 | tf_op jit(solution)/shard_map/ppermute | solution.py:383
  207.9 0.0 all-to-all-done.4
  207.9 7.2 %all-to-all-start.3 = ((bf16[32,160,128]{2,1,0:T(8,128)(2,1)}), bf16[32,160,128]{2,1,0:T(8,128)(2,1)S(1)}, u32[]{:S(2)}, u32[]{:S(2)}) async-start(bf16[32,160,128]{2,1,0:T(8,128)(2,1)} %collective-permute-done.1), calls=%async_computation.3 | async-start | bytes 2621440 | tf_op jit(solution)/shard_map/all_to_all | solution.py:378
  215.2 0.5 sum_parts.1
  215.7 3.8 %collective-permute-start.2 = (bf16[1,128,1024]{2,1,0:T(8,128)(2,1)S(1)}, bf16[1,128,1024]{2,1,0:T(8,128)(2,1)S(1)}, u32[]{:S(2)}, u32[]{:S(2)}) collective-permute-start(bf16[1,128,1024]{2,1,0:T(8,128)(2,1)S(1)} %get-tuple-element.16), channel_id=1, source_target_pairs={{32,0},{64,32},{96,64},{0,96},{33,1},{65,33},{97,65},{1,97},{34,2}... | collective-permute-start | bytes 786440 | tf_op jit(solution)/shard_map/ppermute | solution.py:383
  219.4 0.1 collective-permute-start.3
  219.5 6.6 %collective-permute-done.2 = bf16[1,128,1024]{2,1,0:T(8,128)(2,1)S(1)} collective-permute-done((bf16[1,128,1024]{2,1,0:T(8,128)(2,1)S(1)}, bf16[1,128,1024]{2,1,0:T(8,128)(2,1)S(1)}, u32[]{:S(2)}, u32[]{:S(2)}) %collective-permute-start.2) | collective-permute-done | bytes 262176 | tf_op jit(solution)/shard_map/ppermute | solution.py:383
  226.1 5.0 %collective-permute-done.3 = bf16[1,128,1024]{2,1,0:T(8,128)(2,1)S(1)} collective-permute-done((bf16[1,128,1024]{2,1,0:T(8,128)(2,1)S(1)}, bf16[1,128,1024]{2,1,0:T(8,128)(2,1)S(1)}, u32[]{:S(2)}, u32[]{:S(2)}) %collective-permute-start.3) | collective-permute-done | bytes 262176 | tf_op jit(solution)/shard_map/ppermute | solution.py:383
  231.1 4.7 %all-to-all-done.3 = bf16[32,160,128]{2,1,0:T(8,128)(2,1)S(1)} async-done(((bf16[32,160,128]{2,1,0:T(8,128)(2,1)}), bf16[32,160,128]{2,1,0:T(8,128)(2,1)S(1)}, u32[]{:S(2)}, u32[]{:S(2)}) %all-to-all-start.3) | async-done | bytes 1310752 | tf_op jit(solution)/shard_map/all_to_all | solution.py:378
  235.8 1.3 spread.3
  237.0 0.0 collective-permute-done
  237.0 2.5 %copy.16 = bf16[1,128,5120]{2,1,0:T(8,128)(2,1)} copy(bf16[1,128,5120]{2,1,0:T(8,128)(2,1)} %collective-permute-done) | data formatting | bytes 2621440
  239.5 0.7 copy.17
  240.2 0.7 copy.18
  (15 shorter events, 0.0 us)
Async XLA Ops:
  0.6 1.3 copy-start.6
  1.9 0.9 copy-start.7
  2.9 0.9 copy-start.8
  3.9 0.7 copy-start.9
  4.6 0.7 copy-start.10
  7.4 54.5 %all-to-all-start = ((bf16[32,432,128]{2,1,0:T(8,128)(2,1)}), bf16[32,432,128]{2,1,0:T(8,128)(2,1)S(1)}, u32[]{:S(2)}, u32[]{:S(2)}) async-start(bf16[32,432,128]{2,1,0:T(8,128)(2,1)} %bitcast.1), calls=%async_computation | async-start | bytes 7077888 | tf_op jit(solution)/shard_map/all_to_all | solution.py:378
  15.9 1.3 copy-start.3
  61.9 7.1 %copy-start.16 = (s32[4]{0:T(128)S(1)}, s32[4]{0:T(128)}, u32[]{:S(2)}) copy-start(s32[4]{0:T(128)} %param.15) | copy-start | bytes 52
  61.9 7.2 %copy-start.12 = (s32[20]{0:T(128)S(1)}, s32[20]{0:T(128)}, u32[]{:S(2)}) copy-start(s32[20]{0:T(128)} %constant.10.clone.key_of) | copy-start | bytes 244
  61.9 7.2 %copy-start.13 = (s32[20]{0:T(128)S(1)}, s32[20]{0:T(128)}, u32[]{:S(2)}) copy-start(s32[20]{0:T(128)} %constant.9.clone.row_of) | copy-start | bytes 244
  61.9 54.6 %all-to-all-start.2 = ((bf16[32,160,128]{2,1,0:T(8,128)(2,1)}), bf16[32,160,128]{2,1,0:T(8,128)(2,1)}, u32[]{:S(2)}, u32[]{:S(2)}) async-start(bf16[32,160,128]{2,1,0:T(8,128)(2,1)} %bitcast.3), calls=%async_computation.2 | async-start | bytes 2621440 | tf_op jit(solution)/shard_map/all_to_all | solution.py:378
  112.2 1.9 copy-start
  114.0 1.1 copy-start.4
  115.1 1.5 copy-start.14
  116.6 7.4 %copy-start.5 = (bf16[32,160,128]{2,1,0:T(8,128)(2,1)S(1)}, bf16[32,160,128]{2,1,0:T(8,128)(2,1)}, u32[]{:S(2)}) copy-start(bf16[32,160,128]{2,1,0:T(8,128)(2,1)} %copy-done.4) | copy-start | bytes 3932164
  116.6 52.3 %all-to-all-start.1 = ((bf16[32,160,128]{2,1,0:T(8,128)(2,1)}), bf16[32,160,128]{2,1,0:T(8,128)(2,1)S(1)}, u32[]{:S(2)}, u32[]{:S(2)}) async-start(bf16[32,160,128]{2,1,0:T(8,128)(2,1)} %copy-done.4), calls=%async_computation.1 | async-start | bytes 2621440 | tf_op jit(solution)/shard_map/all_to_all | solution.py:378
  124.0 2.0 copy-start.1
  126.0 1.7 copy-start.15
  166.4 1.4 copy-start.2
  167.8 1.1 copy-start.11
  168.9 39.0 %all-to-all-start.4 = ((bf16[32,256,128]{2,1,0:T(8,128)(2,1)}), bf16[32,256,128]{2,1,0:T(8,128)(2,1)S(1)}, u32[]{:S(2)}, u32[]{:S(2)}) async-start(bf16[32,256,128]{2,1,0:T(8,128)(2,1)} %copy-done.2), calls=%async_computation.4 | async-start | bytes 4194304 | tf_op jit(solution)/shard_map/all_to_all | solution.py:378
  176.3 31.6 %collective-permute-start.1 = (bf16[32,160,128]{2,1,0:T(8,128)(2,1)}, bf16[32,160,128]{2,1,0:T(8,128)(2,1)}, u32[]{:S(2)}, u32[]{:S(2)}) collective-permute-start(bf16[32,160,128]{2,1,0:T(8,128)(2,1)} %copy-done.11), channel_id=1, source_target_pairs={{32,0},{64,32},{96,64},{0,96},{33,1},{65,33},{97,65},{1,97},{34,2}... | collective-permute-start | bytes 3932168 | tf_op jit(solution)/shard_map/ppermute | solution.py:383
  180.4 56.7 %collective-permute-start = (bf16[1,128,5120]{2,1,0:T(8,128)(2,1)}, bf16[1,128,5120]{2,1,0:T(8,128)(2,1)}, u32[]{:S(2)}, u32[]{:S(2)}) collective-permute-start(bf16[1,128,5120]{2,1,0:T(8,128)(2,1)} %spread.2), channel_id=1, source_target_pairs={{96,0},{0,32},{32,64},{64,96},{97,1},{1,33},{33,65},{65,97},{98,2}... | collective-permute-start | bytes 3932168 | tf_op jit(solution)/shard_map/ppermute | solution.py:383
  207.9 27.9 %all-to-all-start.3 = ((bf16[32,160,128]{2,1,0:T(8,128)(2,1)}), bf16[32,160,128]{2,1,0:T(8,128)(2,1)S(1)}, u32[]{:S(2)}, u32[]{:S(2)}) async-start(bf16[32,160,128]{2,1,0:T(8,128)(2,1)} %collective-permute-done.1), calls=%async_computation.3 | async-start | bytes 2621440 | tf_op jit(solution)/shard_map/all_to_all | solution.py:378
  215.7 10.4 %collective-permute-start.2 = (bf16[1,128,1024]{2,1,0:T(8,128)(2,1)S(1)}, bf16[1,128,1024]{2,1,0:T(8,128)(2,1)S(1)}, u32[]{:S(2)}, u32[]{:S(2)}) collective-permute-start(bf16[1,128,1024]{2,1,0:T(8,128)(2,1)S(1)} %get-tuple-element.16), channel_id=1, source_target_pairs={{32,0},{64,32},{96,64},{0,96},{33,1},{65,33},{97,65},{1,97},{34,2}... | collective-permute-start | bytes 786440 | tf_op jit(solution)/shard_map/ppermute | solution.py:383
  219.4 11.6 %collective-permute-start.3 = (bf16[1,128,1024]{2,1,0:T(8,128)(2,1)S(1)}, bf16[1,128,1024]{2,1,0:T(8,128)(2,1)S(1)}, u32[]{:S(2)}, u32[]{:S(2)}) collective-permute-start(bf16[1,128,1024]{2,1,0:T(8,128)(2,1)S(1)} %get-tuple-element.17), channel_id=1, source_target_pairs={{32,0},{64,32},{96,64},{0,96},{33,1},{65,33},{97,65},{1,97},{34,2}... | collective-permute-start | bytes 786440 | tf_op jit(solution)/shard_map/ppermute | solution.py:383

commit v3 on v2

--- a/solution.py
+++ b/solution.py
@@ -19,10 +19,11 @@
 K0, V0, P0 = QR, QR + TOK, QR + 2 * TOK
 PACK = P0 + 2 * PRE
 RC = 8
-KC = 4
+KC = 8
 M = RC * QR
 N = KC * TOK
 HALF = M // 2
+FULL = HALF
 N_RB = CHUNKS // RC
 PTOT = CHUNKS * PRE
 SCALE = 1.0 / math.sqrt(HD)
@@ -30,18 +31,22 @@
 NEG = -1e30
 F32 = jnp.float32
 BF16 = jnp.bfloat16
-VMEM = 40 * 2**20
-
-ROW_OF = np.array([r for r in reversed(range(N_RB)) for _ in range(2 * r + 2)], np.int32)
-KEY_OF = np.array([k for r in reversed(range(N_RB)) for k in range(2 * r + 2)], np.int32)
+VMEM = 56 * 2**20
+
+ROW_OF = np.array([r for r in reversed(range(N_RB)) for _ in range(r + 1)], np.int32)
+KEY_OF = np.array([k for r in reversed(range(N_RB)) for k in range(r + 1)], np.int32)
 STEPS = len(ROW_OF)
 
 
 def COST(products):
-    entries = (STEPS + N_RB) * M * N
+    entries = STEPS * M * N
     return pl.CostEstimate(
         flops=products * 2 * entries * HD, transcendentals=entries, bytes_accessed=products * entries
     )
+
+
+def in_hbm(*arrays):
+    return tuple(pltpu.with_memory_space_constraint(x, pltpu.HBM) for x in arrays)
 
 
 def dot(a, b, ca, cb):
@@ -115,42 +120,37 @@
                 shift[...] = jnp.maximum(shift[...], top)
                 return carry
 
-            lax.fori_loop(0, 2 * rb + 2, step, 0)
-
-    def tile(first, keys, values, live=None, at=None):
+            lax.fori_loop(0, rb + 1, step, 0)
+
+    def tile(first, rows, keys, values, live=None, at=None):
         width = keys.shape[0]
         row, col = at or (first, 0)
-        q = pack[pl.ds(rb * RC + first // QR, RC // 2), 0:QR, :].reshape(HALF, HD)
-        e = jnp.exp(dot(q, keys, 1, 1) * SCALE - wide(shift[first : first + HALF, :], width))
+        q = pack[pl.ds(rb * RC + first // QR, rows // QR), 0:QR, :].reshape(rows, HD)
+        e = jnp.exp(dot(q, keys, 1, 1) * SCALE - wide(shift[first : first + rows, :], width))
         if live is not None:
             e = jnp.where(live, e, 0.0)
         e = e.astype(BF16)
-        e_out[0, row : row + HALF, col : col + width] = e
+        e_out[0, row : row + rows, col : col + width] = e
         both = jnp.concatenate([values, jnp.ones_like(values)], axis=1)
-        acc[first : first + HALF, :] += dot(e, both, 1, 0)
+        acc[first : first + rows, :] += dot(e, both, 1, 0)
 
     keys = pack[pl.ds(kb * KC, KC), K0:V0, :].reshape(N, HD)
     values = pack[pl.ds(kb * KC, KC), V0:P0, :].reshape(N, HD)
-    causal = lambda: key_pos(HALF, N) <= row_pos(RC // 2, N, part)
-
-    @pl.when(kb < 2 * rb)
-    def _():
-        tile(0, keys, values)
-
-    @pl.when(kb <= 2 * rb)
-    def _():
-        tile(HALF, keys, values)
-
-    @pl.when(kb == 2 * rb)
-    def _():
-        tile(0, keys, values, causal())
-
-    @pl.when(kb == 2 * rb + 1)
-    def _():
-        tile(HALF, keys, values, causal())
+
+    @pl.when(kb < rb)
+    def _():
+        for first in range(0, M, FULL):
+            tile(first, FULL, keys, values)
+
+    @pl.when(kb == rb)
+    def _():
+        half = N // 2
+        pos = row_pos(RC // 2, half, part)
+        tile(0, HALF, keys[:half], values[:half], key_pos(HALF, half) <= pos)
+        tile(HALF, HALF, keys, values, key_pos(HALF, N) <= wide(pos, N) + half)
         live = prefix_live(meta, HALF)
-        for half in range(2):
-            tile(half * HALF, pk[...], pv[...], live, (0, half * PTOT))
+        for i in range(2):
+            tile(i * HALF, HALF, pk[...], pv[...], live, (0, half + i * PTOT))
         inverse = 1.0 / acc[:, HD:]
         li_out[...] = inverse
         o_out[...] = (acc[:, :HD] * inverse).astype(BF16).reshape(RC, QR, HD)
@@ -162,7 +162,7 @@
         grid_spec=pltpu.PrefetchScalarGridSpec(
             num_scalar_prefetch=3,
             grid=(STEPS,),
-            in_specs=[pl.BlockSpec(memory_space=pltpu.VMEM)],
+            in_specs=[pl.BlockSpec((CHUNKS, PACK, HD), lambda t, r, k, m: (0, 0, 0))],
             out_specs=[
                 pl.BlockSpec((1, M, N), lambda t, r, k, m: (t, 0, 0)),
                 pl.BlockSpec((RC, QR, HD), lambda t, r, k, m: (r[t], 0, 0)),
@@ -177,14 +177,14 @@
             ],
         ),
         out_shape=[
-            jax.ShapeDtypeStruct((STEPS, M, N), BF16),
-            jax.ShapeDtypeStruct((CHUNKS, QR, HD), BF16),
-            jax.ShapeDtypeStruct((N_RB * M, HD), F32),
+            pltpu.HBM((STEPS, M, N), BF16),
+            pltpu.HBM((CHUNKS, QR, HD), BF16),
+            pltpu.HBM((N_RB * M, HD), F32),
         ],
         compiler_params=pltpu.CompilerParams(vmem_limit_bytes=VMEM),
         cost_estimate=COST(2),
         name="forward",
-    )(jnp.asarray(ROW_OF), jnp.asarray(KEY_OF), meta, pack)
+    )(jnp.asarray(ROW_OF), jnp.asarray(KEY_OF), meta, *in_hbm(pack))
 
 
 def backward_kernel(row_of, key_of, meta, pack, d_in, e_in, o_in, li_in, dq_out, dkv_out, dq, dk, dv, dn, delta, pk, pv):
@@ -212,36 +212,36 @@
         dk[here, :] = jnp.zeros((N, HD), F32)
         dv[here, :] = jnp.zeros((N, HD), F32)
 
-    def tile(first, keys, values, at=None):
+    def tile(first, rows, keys, values, at=None):
         width = keys.shape[0]
         row, col = at or (first, 0)
-        d = dn[first : first + HALF, :]
-        e = e_in[0, row : row + HALF, col : col + width]
-        dp = dot(d, values, 1, 1) - wide(delta[first : first + HALF, :], width)
+        d = dn[first : first + rows, :]
+        e = e_in[0, row : row + rows, col : col + width]
+        dp = dot(d, values, 1, 1) - wide(delta[first : first + rows, :], width)
         ds = (e.astype(F32) * dp).astype(BF16)
-        dq[first : first + HALF, :] += dot(ds, keys, 1, 0)
+        dq[first : first + rows, :] += dot(ds, keys, 1, 0)
         if at is None:
-            q = pack[pl.ds(rb * RC + first // QR, RC // 2), 0:QR, :].reshape(HALF, HD)
-            dv[here, :] += dot(e, d, 0, 0)
-            dk[here, :] += dot(ds, q, 0, 0)
+            q = pack[pl.ds(rb * RC + first // QR, rows // QR), 0:QR, :].reshape(rows, HD)
+            to = pl.ds(kb * N, width)
+            dv[to, :] += dot(e, d, 0, 0)
+            dk[to, :] += dot(ds, q, 0, 0)
 
     keys = pack[pl.ds(kb * KC, KC), K0:V0, :].reshape(N, HD)
     values = pack[pl.ds(kb * KC, KC), V0:P0, :].reshape(N, HD)
 
-    @pl.when(kb <= 2 * rb)
-    def _():
-        tile(0, keys, values)
-
-    tile(HALF, keys, values)
-
-    @pl.when(kb == 2 * rb + 1)
-    def _():
-        for half in range(2):
-            tile(half * HALF, pk[...], pv[...], (0, half * PTOT))
+    @pl.when(kb < rb)
+    def _():
+        for first in range(0, M, FULL):
+            tile(first, FULL, keys, values)
+
+    @pl.when(kb == rb)
+    def _():
+        half = N // 2
+        tile(0, HALF, keys[:half], values[:half])
+        tile(HALF, HALF, keys, values)
+        for i in range(2):
+            tile(i * HALF, HALF, pk[...], pv[...], (0, half + i * PTOT))
         dq_out[...] = dq[...].astype(BF16).reshape(RC, QR, HD)
-
-    @pl.when(kb >= 2 * rb)
-    def _():
         dkv_out[:, 0:TOK, :] = dk[here, :].astype(BF16).reshape(KC, TOK, HD)
         dkv_out[:, TOK:, :] = (dv[here, :] * (1.0 / SCALE)).astype(BF16).reshape(KC, TOK, HD)
 
@@ -254,7 +254,7 @@
             num_scalar_prefetch=3,
             grid=(STEPS,),
             in_specs=[
-                pl.BlockSpec(memory_space=pltpu.VMEM),
+                pl.BlockSpec((CHUNKS, PACK, HD), lambda t, r, k, m: (0, 0, 0)),
                 by_rows(RC, QR, HD),
                 pl.BlockSpec((1, M, N), lambda t, r, k, m: (t, 0, 0)),
                 by_rows(RC, QR, HD),
@@ -262,7 +262,7 @@
             ],
             out_specs=[
                 by_rows(RC, QR, HD),
-                pl.BlockSpec((KC, 2 * TOK, HD), lambda t, r, k, m: (jnp.maximum(k[t], 2 * r[t]), 0, 0)),
+                by_rows(KC, 2 * TOK, HD),
             ],
             scratch_shapes=[
                 pltpu.VMEM((M, HD), F32),
@@ -275,13 +275,13 @@
             ],
         ),
         out_shape=[
-            jax.ShapeDtypeStruct((CHUNKS, QR, HD), BF16),
-            jax.ShapeDtypeStruct((CHUNKS, 2 * TOK, HD), BF16),
+            pltpu.HBM((CHUNKS, QR, HD), BF16),
+            pltpu.HBM((CHUNKS, 2 * TOK, HD), BF16),
         ],
         compiler_params=pltpu.CompilerParams(vmem_limit_bytes=VMEM),
         cost_estimate=COST(4),
         name="backward",
-    )(jnp.asarray(ROW_OF), jnp.asarray(KEY_OF), meta, pack, d, e, o, li)
+    )(jnp.asarray(ROW_OF), jnp.asarray(KEY_OF), meta, *in_hbm(pack, d, e, o, li))
 
 
 GROUPS = CHUNKS // SPLIT
@@ -327,10 +327,10 @@
         grid=(GROUPS // AT_ONCE,),
         in_specs=[cols(x.shape[1], x.shape[2] // GROUPS) for x in (queries,) + rest],
         out_specs=parts_of(rows),
-        out_shape=jax.ShapeDtypeStruct((SPLIT, GROUPS, rows, HD), BF16),
+        out_shape=pltpu.HBM((SPLIT, GROUPS, rows, HD), BF16),
         compiler_params=pltpu.CompilerParams(vmem_limit_bytes=VMEM),
         name="gather",
-    )(queries, *rest)
+    )(*in_hbm(queries, *rest))
     return packed.reshape(CHUNKS, rows, HD)
 
 
@@ -346,10 +346,10 @@
         grid=(GROUPS // AT_ONCE,),
         in_specs=[parts_of(QR)],
         out_specs=cols(TOK, GROUP * HD),
-        out_shape=jax.ShapeDtypeStruct((1, TOK, GROUPS * GROUP * HD), BF16),
+        out_shape=pltpu.HBM((1, TOK, GROUPS * GROUP * HD), BF16),
         compiler_params=pltpu.CompilerParams(vmem_limit_bytes=VMEM),
         name="spread",
-    )(packed.reshape(SPLIT, GROUPS, QR, HD))
+    )(*in_hbm(packed.reshape(SPLIT, GROUPS, QR, HD)))
 
 
 def sum_kernel(parts, keys, values):
@@ -362,7 +362,7 @@
 
 
 def sum_parts(parts):
-    shape = jax.ShapeDtypeStruct((1, TOK, GROUPS * HD), BF16)
+    shape = pltpu.HBM((1, TOK, GROUPS * HD), BF16)
     return pl.pallas_call(
         sum_kernel,
         grid=(GROUPS // AT_ONCE,),
@@ -371,7 +371,7 @@
         out_shape=[shape, shape],
         compiler_params=pltpu.CompilerParams(vmem_limit_bytes=VMEM),
         name="sum_parts",
-    )(parts.reshape(SPLIT, GROUPS, 2 * TOK, HD))
+    )(*in_hbm(parts.reshape(SPLIT, GROUPS, 2 * TOK, HD)))
 
 
 def exchange(x):
@@ -388,11 +388,12 @@
     meta = jnp.concatenate([prefix_fill, part[None]])
     pack = exchange(gather(queries, keys, values, pre_keys, pre_values))
     d = exchange(gather(d_out))
-    pack = pltpu.with_memory_space_constraint(pack, pltpu.VMEM)
     e, o, li = forward(meta, pack)
-    next_input = shifted(spread(exchange(o)), 1)
+    moved_o = shifted(exchange(o), 1)
     dq, dkv = backward(meta, pack, d, e, o, li)
-    query_grad = spread(exchange(shifted(dq, -1)))
+    moved_dq, moved_o = lax.optimization_barrier((shifted(dq, -1), moved_o))
+    query_grad = spread(exchange(moved_dq))
+    next_input = spread(moved_o)
     key_grad, value_grad = (shifted(x, -1) for x in sum_parts(exchange(dkv)))
     return (next_input, query_grad, key_grad, value_grad)
 

time: 243 us -> 227 us (0.934)
  local copies, waits for them, and re-layouts: 20.4 us -> 4.87 us
  waiting for transfers between devices: 87.3 us -> 90.7 us
  starting transfers between devices: 44.2 us -> 41.5 us
    unnamed x37 -> x14, local copies, waits for them, and re-layouts: 20.4 us -> 4.87 us
    ppermute x4, waiting for transfers between devices: 39.1 us -> 45.2 us  [shifted(): lax.ppermute(block, 'section', [((i - distance) % count, i) for i in rang...]
    pallas_call x1, Pallas kernels: 43 us -> 38.2 us  [forward(): pl.pallas_call(forward_kernel, grid_spec=pltpu.PrefetchScalarGridSpec(num...]
    all_to_all x5, waiting for transfers between devices: 48.2 us -> 45.5 us  [exchange(): lax.all_to_all(x, ('blk', 'uly'), split_axis=0, concat_axis=0, tiled=True)]
    ppermute x4, starting transfers between devices: 6.67 us -> 4.11 us  [shifted(): lax.ppermute(block, 'section', [((i - distance) % count, i) for i in rang...]
  transfers between devices with their start and end apart: 9 -> 9, of which waited for: 5 -> 6; matrix products, arithmetic and copies ran while one was open for 0% -> 0% of each run, Pallas kernels for 36% -> 36%
where the time goes in v3:
time: 227 us; the launch traced here: 226 us
  waiting for transfers between devices  90.7 us (40%)
  Pallas kernels  87.6 us (39%)
  starting transfers between devices  41.5 us (18%)
  local copies, waits for them, and re-layouts  4.87 us (2%)
    all_to_all x5, waiting for transfers between devices, exchange(): lax.all_to_all(x, ('blk', 'uly'), split_axis=0, concat_axis=0, tiled=True)  45.5 us
    ppermute x4, waiting for transfers between devices, shifted(): lax.ppermute(block, 'section', [((i - distance) % count, i) for i in rang...  45.2 us
    pallas_call x1, Pallas kernels, forward(): pl.pallas_call(forward_kernel, grid_spec=pltpu.PrefetchScalarGridSpec(num...  38.2 us
    all_to_all x5, starting transfers between devices, exchange(): lax.all_to_all(x, ('blk', 'uly'), split_axis=0, concat_axis=0, tiled=True)  37.4 us
    pallas_call x1, Pallas kernels, backward(): pl.pallas_call(backward_kernel, grid_spec=pltpu.PrefetchScalarGridSpec(nu...  37.1 us
    pallas_call x2, Pallas kernels, gather(): pl.pallas_call(gather_kernel, grid=(GROUPS // AT_ONCE,), in_specs=[cols(x...  5.47 us
    unnamed x14, local copies, waits for them, and re-layouts  4.87 us
  transfers between devices with their start and end apart: 9, of which 6 were waited for; matrix products, arithmetic and copies ran while one was open for 0% of the time, Pallas kernels for 36%

profile of v3, /device:TPU:0, one launch (start us, length us, event | category | flops | bytes accessed | tf_op | source)
XLA Modules:
  0.0 226.0 jit_solution(15152045356255512772)
XLA Ops:
  0.6 3.2 %gather.2 = bf16[4,8,432,128]{3,2,1,0:T(8,128)(2,1)} custom-call(bf16[1,128,5120]{2,1,0:T(8,128)(2,1)} %refs_0_.2, bf16[1,128,1024]{2,1,0:T(8,128)(2,1)} %refs_1_.1, bf16[1,128,1024]{2,1,0:T(8,128)(2,1)} %refs_2_.1, bf16[1,8,1024]{2,1,0:T(8,128)(2,1)} %refs_3_.1, bf16[1,8,1024]{2,1,0:T(8,128)(2,1)} %refs_4_.1), custom_call_target="tpu_custom_call" | custom-call | tf_op jit(solution)/shard_map/gather/pallas_call | solution.py:325
  3.8 8.4 %all-to-all-start = ((bf16[32,432,128]{2,1,0:T(8,128)(2,1)}), bf16[32,432,128]{2,1,0:T(8,128)(2,1)S(1)}, u32[]{:S(2)}, u32[]{:S(2)}) async-start(bf16[32,432,128]{2,1,0:T(8,128)(2,1)} %bitcast.6), calls=%async_computation | async-start | bytes 7077888 | tf_op jit(solution)/shard_map/all_to_all | solution.py:378
  12.3 2.3 %gather.3 = bf16[4,8,160,128]{3,2,1,0:T(8,128)(2,1)} custom-call(bf16[1,128,5120]{2,1,0:T(8,128)(2,1)} %refs_0_.3), custom_call_target="tpu_custom_call" | custom-call | tf_op jit(solution)/shard_map/gather/pallas_call | solution.py:325
  14.5 43.8 %all-to-all-done.pack = bf16[32,432,128]{2,1,0:T(8,128)(2,1)S(1)} async-done(((bf16[32,432,128]{2,1,0:T(8,128)(2,1)}), bf16[32,432,128]{2,1,0:T(8,128)(2,1)S(1)}, u32[]{:S(2)}, u32[]{:S(2)}) %all-to-all-start) | async-done | bytes 3538976 | tf_op jit(solution)/shard_map/all_to_all | solution.py:378
  58.3 0.0 copy-start.2
  58.3 0.0 copy-start.5
  58.3 7.1 %all-to-all-start.1 = ((bf16[32,160,128]{2,1,0:T(8,128)(2,1)}), bf16[32,160,128]{2,1,0:T(8,128)(2,1)}, u32[]{:S(2)}, u32[]{:S(2)}) async-start(bf16[32,160,128]{2,1,0:T(8,128)(2,1)} %bitcast.9), calls=%async_computation.1 | async-start | bytes 2621440 | tf_op jit(solution)/shard_map/all_to_all | solution.py:378
  65.4 0.0 copy-done.5
  65.4 0.6 pad_add_fusion.meta
  66.0 0.0 copy-done.2
  66.0 38.2 %forward.1 = (bf16[10,1280,1024]{2,1,0:T(8,128)(2,1)}, bf16[32,160,128]{2,1,0:T(8,128)(2,1)}, f32[5120,128]{1,0:T(8,128)}) custom-call(s32[10]{0:T(128)} %constant.9.clone.row_of, s32[10]{0:T(128)} %constant.10.clone.key_of, s32[5]{0:T(128)} %pad_add_fusion.meta, bf16[32,432,128]{2,1,0:T(8,128)(2,1)} %copy-done.2), custom_call_target="tpu_custom_call" | custom-call | flops 6710886400 | bytes 26214400 | tf_op jit(solution)/shard_map/forward/pallas_call | solution.py:160
  104.2 0.0 all-to-all-done.1.d_in
  104.2 7.5 %all-to-all-start.2 = ((bf16[32,160,128]{2,1,0:T(8,128)(2,1)}), bf16[32,160,128]{2,1,0:T(8,128)(2,1)S(1)}, u32[]{:S(2)}, u32[]{:S(2)}) async-start(bf16[32,160,128]{2,1,0:T(8,128)(2,1)} %get-tuple-element.14.o_in), calls=%async_computation.2 | async-start | bytes 2621440 | tf_op jit(solution)/shard_map/all_to_all | solution.py:378
  111.7 37.1 %backward.1 = (bf16[32,160,128]{2,1,0:T(8,128)(2,1)}, bf16[32,256,128]{2,1,0:T(8,128)(2,1)}) custom-call(s32[10]{0:T(128)} %constant.9.clone.row_of, s32[10]{0:T(128)} %constant.10.clone.key_of, s32[5]{0:T(128)} %pad_add_fusion.meta, bf16[32,432,128]{2,1,0:T(8,128)(2,1)} %copy-done.2, bf16[32,160,128]{2,1,0:T(8,128)(2,1)} %all-to-all-done.1.d_in, ...), custom_call_target="tpu_custom_call" | custom-call | flops 13421772800 | bytes 52428800 | tf_op jit(solution)/shard_map/backward/pallas_call | solution.py:251
  148.8 0.0 all-to-all-done.2
  148.8 0.0 copy-start.4
  148.8 1.0 copy-done.4
  149.9 7.2 %all-to-all-start.4 = ((bf16[32,256,128]{2,1,0:T(8,128)(2,1)}), bf16[32,256,128]{2,1,0:T(8,128)(2,1)S(1)}, u32[]{:S(2)}, u32[]{:S(2)}) async-start(bf16[32,256,128]{2,1,0:T(8,128)(2,1)} %get-tuple-element.19), calls=%async_computation.4 | async-start | bytes 4194304 | tf_op jit(solution)/shard_map/all_to_all | solution.py:378
  157.1 2.8 %collective-permute-start = (bf16[32,160,128]{2,1,0:T(8,128)(2,1)}, bf16[32,160,128]{2,1,0:T(8,128)(2,1)S(1)}, u32[]{:S(2)}, u32[]{:S(2)}) collective-permute-start(bf16[32,160,128]{2,1,0:T(8,128)(2,1)} %get-tuple-element.16), channel_id=1, source_target_pairs={{32,0},{64,32},{96,64},{0,96},{33,1},{65,33},{97,65},{1,97},{34,2}... | collective-permute-start | bytes 3932168 | tf_op jit(solution)/shard_map/ppermute | solution.py:383
  159.9 0.0 collective-permute-start.1
  159.9 28.8 %collective-permute-done = bf16[32,160,128]{2,1,0:T(8,128)(2,1)S(1)} collective-permute-done((bf16[32,160,128]{2,1,0:T(8,128)(2,1)}, bf16[32,160,128]{2,1,0:T(8,128)(2,1)S(1)}, u32[]{:S(2)}, u32[]{:S(2)}) %collective-permute-start) | collective-permute-done | bytes 1310752 | tf_op jit(solution)/shard_map/ppermute | solution.py:383
  188.7 0.0 copy-start.3
  188.7 3.4 %collective-permute-done.1 = bf16[32,160,128]{2,1,0:T(8,128)(2,1)} collective-permute-done((bf16[32,160,128]{2,1,0:T(8,128)(2,1)}, bf16[32,160,128]{2,1,0:T(8,128)(2,1)}, u32[]{:S(2)}, u32[]{:S(2)}) %collective-permute-start.1) | collective-permute-done | bytes 1310752 | tf_op jit(solution)/shard_map/ppermute | solution.py:383
  192.1 0.0 copy-done.3
  192.1 0.0 all-to-all-done.4
  192.1 0.0 copy-start
  192.1 1.3 copy-done
  193.4 7.2 %all-to-all-start.3 = ((bf16[32,160,128]{2,1,0:T(8,128)(2,1)}), bf16[32,160,128]{2,1,0:T(8,128)(2,1)S(1)}, u32[]{:S(2)}, u32[]{:S(2)}) async-start(bf16[32,160,128]{2,1,0:T(8,128)(2,1)} %copy-done.3), calls=%async_computation.3 | async-start | bytes 2621440 | tf_op jit(solution)/shard_map/all_to_all | solution.py:378
  200.7 2.4 %sum_parts.1 = (bf16[1,128,1024]{2,1,0:T(8,128)(2,1)}, bf16[1,128,1024]{2,1,0:T(8,128)(2,1)}) custom-call(bf16[4,8,256,128]{3,2,1,0:T(8,128)(2,1)} %bitcast.7), custom_call_target="tpu_custom_call" | custom-call | tf_op jit(solution)/shard_map/sum_parts/pallas_call | solution.py:366
  203.1 1.2 collective-permute-start.2
  204.3 0.0 collective-permute-start.3
  204.3 8.1 %collective-permute-done.2 = bf16[1,128,1024]{2,1,0:T(8,128)(2,1)S(1)} collective-permute-done((bf16[1,128,1024]{2,1,0:T(8,128)(2,1)}, bf16[1,128,1024]{2,1,0:T(8,128)(2,1)S(1)}, u32[]{:S(2)}, u32[]{:S(2)}) %collective-permute-start.2) | collective-permute-done | bytes 262176 | tf_op jit(solution)/shard_map/ppermute | solution.py:383
  212.4 5.0 %collective-permute-done.3 = bf16[1,128,1024]{2,1,0:T(8,128)(2,1)S(1)} collective-permute-done((bf16[1,128,1024]{2,1,0:T(8,128)(2,1)}, bf16[1,128,1024]{2,1,0:T(8,128)(2,1)S(1)}, u32[]{:S(2)}, u32[]{:S(2)}) %collective-permute-start.3) | collective-permute-done | bytes 262176 | tf_op jit(solution)/shard_map/ppermute | solution.py:383
  217.4 2.3 spread.2
  219.6 1.7 all-to-all-done.3
  221.3 0.0 copy-start.1
  221.3 1.1 copy-done.1
  222.4 2.3 spread.3
  224.6 0.7 copy.15
  225.3 0.7 copy.16
Async XLA Ops:
  3.8 54.5 %all-to-all-start = ((bf16[32,432,128]{2,1,0:T(8,128)(2,1)}), bf16[32,432,128]{2,1,0:T(8,128)(2,1)S(1)}, u32[]{:S(2)}, u32[]{:S(2)}) async-start(bf16[32,432,128]{2,1,0:T(8,128)(2,1)} %bitcast.6), calls=%async_computation | async-start | bytes 7077888 | tf_op jit(solution)/shard_map/all_to_all | solution.py:378
  58.3 7.7 %copy-start.2 = (bf16[32,432,128]{2,1,0:T(8,128)(2,1)}, bf16[32,432,128]{2,1,0:T(8,128)(2,1)S(1)}, u32[]{:S(2)}) copy-start(bf16[32,432,128]{2,1,0:T(8,128)(2,1)S(1)} %all-to-all-done.pack) | copy-start | bytes 10616836
  58.3 7.1 %copy-start.5 = (s32[4]{0:T(128)S(1)}, s32[4]{0:T(128)}, u32[]{:S(2)}) copy-start(s32[4]{0:T(128)} %param.15) | copy-start | bytes 52
  58.3 45.9 %all-to-all-start.1 = ((bf16[32,160,128]{2,1,0:T(8,128)(2,1)}), bf16[32,160,128]{2,1,0:T(8,128)(2,1)}, u32[]{:S(2)}, u32[]{:S(2)}) async-start(bf16[32,160,128]{2,1,0:T(8,128)(2,1)} %bitcast.9), calls=%async_computation.1 | async-start | bytes 2621440 | tf_op jit(solution)/shard_map/all_to_all | solution.py:378
  104.2 44.6 %all-to-all-start.2 = ((bf16[32,160,128]{2,1,0:T(8,128)(2,1)}), bf16[32,160,128]{2,1,0:T(8,128)(2,1)S(1)}, u32[]{:S(2)}, u32[]{:S(2)}) async-start(bf16[32,160,128]{2,1,0:T(8,128)(2,1)} %get-tuple-element.14.o_in), calls=%async_computation.2 | async-start | bytes 2621440 | tf_op jit(solution)/shard_map/all_to_all | solution.py:378
  148.8 1.1 copy-start.4
  149.9 42.2 %all-to-all-start.4 = ((bf16[32,256,128]{2,1,0:T(8,128)(2,1)}), bf16[32,256,128]{2,1,0:T(8,128)(2,1)S(1)}, u32[]{:S(2)}, u32[]{:S(2)}) async-start(bf16[32,256,128]{2,1,0:T(8,128)(2,1)} %get-tuple-element.19), calls=%async_computation.4 | async-start | bytes 4194304 | tf_op jit(solution)/shard_map/all_to_all | solution.py:378
  157.1 31.6 %collective-permute-start = (bf16[32,160,128]{2,1,0:T(8,128)(2,1)}, bf16[32,160,128]{2,1,0:T(8,128)(2,1)S(1)}, u32[]{:S(2)}, u32[]{:S(2)}) collective-permute-start(bf16[32,160,128]{2,1,0:T(8,128)(2,1)} %get-tuple-element.16), channel_id=1, source_target_pairs={{32,0},{64,32},{96,64},{0,96},{33,1},{65,33},{97,65},{1,97},{34,2}... | collective-permute-start | bytes 3932168 | tf_op jit(solution)/shard_map/ppermute | solution.py:383
  159.9 32.2 %collective-permute-start.1 = (bf16[32,160,128]{2,1,0:T(8,128)(2,1)}, bf16[32,160,128]{2,1,0:T(8,128)(2,1)}, u32[]{:S(2)}, u32[]{:S(2)}) collective-permute-start(bf16[32,160,128]{2,1,0:T(8,128)(2,1)} %copy-done.4), channel_id=1, source_target_pairs={{96,0},{0,32},{32,64},{64,96},{97,1},{1,33},{33,65},{65,97},{98,2}... | collective-permute-start | bytes 3932168 | tf_op jit(solution)/shard_map/ppermute | solution.py:383
  188.7 3.4 %copy-start.3 = (bf16[32,160,128]{2,1,0:T(8,128)(2,1)}, bf16[32,160,128]{2,1,0:T(8,128)(2,1)S(1)}, u32[]{:S(2)}) copy-start(bf16[32,160,128]{2,1,0:T(8,128)(2,1)S(1)} %collective-permute-done) | copy-start | bytes 3932164
  192.1 1.3 copy-start
  193.4 27.9 %all-to-all-start.3 = ((bf16[32,160,128]{2,1,0:T(8,128)(2,1)}), bf16[32,160,128]{2,1,0:T(8,128)(2,1)S(1)}, u32[]{:S(2)}, u32[]{:S(2)}) async-start(bf16[32,160,128]{2,1,0:T(8,128)(2,1)} %copy-done.3), calls=%async_computation.3 | async-start | bytes 2621440 | tf_op jit(solution)/shard_map/all_to_all | solution.py:378
  203.1 9.3 %collective-permute-start.2 = (bf16[1,128,1024]{2,1,0:T(8,128)(2,1)}, bf16[1,128,1024]{2,1,0:T(8,128)(2,1)S(1)}, u32[]{:S(2)}, u32[]{:S(2)}) collective-permute-start(bf16[1,128,1024]{2,1,0:T(8,128)(2,1)} %get-tuple-element.20), channel_id=1, source_target_pairs={{32,0},{64,32},{96,64},{0,96},{33,1},{65,33},{97,65},{1,97},{34,2}... | collective-permute-start | bytes 786440 | tf_op jit(solution)/shard_map/ppermute | solution.py:383
  204.3 13.1 %collective-permute-start.3 = (bf16[1,128,1024]{2,1,0:T(8,128)(2,1)}, bf16[1,128,1024]{2,1,0:T(8,128)(2,1)S(1)}, u32[]{:S(2)}, u32[]{:S(2)}) collective-permute-start(bf16[1,128,1024]{2,1,0:T(8,128)(2,1)} %get-tuple-element.21), channel_id=1, source_target_pairs={{32,0},{64,32},{96,64},{0,96},{33,1},{65,33},{97,65},{1,97},{34,2}... | collective-permute-start | bytes 786440 | tf_op jit(solution)/shard_map/ppermute | solution.py:383
  221.3 1.1 copy-start.1

commit v4 on v3

--- a/solution.py
+++ b/solution.py
@@ -16,7 +16,7 @@
 SUB = TOK // SPLIT
 QR = GROUP * SUB
 PRE = 8
-K0, V0, P0 = QR, QR + TOK, QR + 2 * TOK
+K0, P0 = QR, QR + TOK
 PACK = P0 + 2 * PRE
 RC = 8
 KC = 8
@@ -85,7 +85,19 @@
     return both[:, which * PRE : (which + 1) * PRE].reshape(PTOT, HD).astype(BF16)
 
 
-def forward_kernel(row_of, key_of, meta, pack, e_out, o_out, li_out, acc, shift, pk, pv, knorm):
+def keys_and_values(part, pack, other, kall, vall):
+    @pl.when(part % 2 == 0)
+    def _():
+        kall[...] = pack[:, K0:P0, :]
+        vall[...] = other[...]
+
+    @pl.when(part % 2 == 1)
+    def _():
+        kall[...] = other[...]
+        vall[...] = pack[:, K0:P0, :]
+
+
+def forward_kernel(row_of, key_of, meta, pack, other, e_out, o_out, li_out, acc, shift, pk, pv, kall, vall, knorm):
     t = pl.program_id(0)
     rb, kb = row_of[t], key_of[t]
     part = meta[SPLIT]
@@ -94,7 +106,8 @@
     def _():
         pk[...] = prefix_rows(pack, 0)
         pv[...] = prefix_rows(pack, 1)
-        knorm[0] = jnp.maximum(row_norm(pk[...]), row_norm(pack[:, K0:V0, :].reshape(CHUNKS * TOK, HD)))
+        keys_and_values(part, pack, other, kall, vall)
+        knorm[0] = jnp.maximum(row_norm(pk[...]), row_norm(kall[...].reshape(CHUNKS * TOK, HD)))
 
     def queries():
         return pack[pl.ds(rb * RC, RC), 0:QR, :].reshape(M, HD)
@@ -113,7 +126,7 @@
             shift[...] = jnp.broadcast_to(jnp.max(s, axis=1, keepdims=True), shift.shape)
 
             def step(k, carry):
-                keys = pack[pl.ds(k * KC, KC), K0:V0, :].reshape(N, HD)
+                keys = kall[pl.ds(k * KC, KC)].reshape(N, HD)
                 pos = row_pos(RC, N, part) + rb * (RC * TOK)
                 s = jnp.where(key_pos(M, N) + k * N <= pos, dot(q, keys, 1, 1) * SCALE, NEG)
                 top = jnp.broadcast_to(jnp.max(s, axis=1, keepdims=True), shift.shape)
@@ -134,8 +147,8 @@
         both = jnp.concatenate([values, jnp.ones_like(values)], axis=1)
         acc[first : first + rows, :] += dot(e, both, 1, 0)
 
-    keys = pack[pl.ds(kb * KC, KC), K0:V0, :].reshape(N, HD)
-    values = pack[pl.ds(kb * KC, KC), V0:P0, :].reshape(N, HD)
+    keys = kall[pl.ds(kb * KC, KC)].reshape(N, HD)
+    values = vall[pl.ds(kb * KC, KC)].reshape(N, HD)
 
     @pl.when(kb < rb)
     def _():
@@ -156,13 +169,16 @@
         o_out[...] = (acc[:, :HD] * inverse).astype(BF16).reshape(RC, QR, HD)
 
 
-def forward(meta, pack):
+def forward(meta, pack, other):
     return pl.pallas_call(
         forward_kernel,
         grid_spec=pltpu.PrefetchScalarGridSpec(
             num_scalar_prefetch=3,
             grid=(STEPS,),
-            in_specs=[pl.BlockSpec((CHUNKS, PACK, HD), lambda t, r, k, m: (0, 0, 0))],
+            in_specs=[
+                pl.BlockSpec((CHUNKS, PACK, HD), lambda t, r, k, m: (0, 0, 0)),
+                pl.BlockSpec((CHUNKS, TOK, HD), lambda t, r, k, m: (0, 0, 0)),
+            ],
             out_specs=[
                 pl.BlockSpec((1, M, N), lambda t, r, k, m: (t, 0, 0)),
                 pl.BlockSpec((RC, QR, HD), lambda t, r, k, m: (r[t], 0, 0)),
@@ -173,6 +189,8 @@
                 pltpu.VMEM((M, HD), F32),
                 pltpu.VMEM((PTOT, HD), BF16),
                 pltpu.VMEM((PTOT, HD), BF16),
+                pltpu.VMEM((CHUNKS, TOK, HD), BF16),
+                pltpu.VMEM((CHUNKS, TOK, HD), BF16),
                 pltpu.SMEM((1,), F32),
             ],
         ),
@@ -184,10 +202,10 @@
         compiler_params=pltpu.CompilerParams(vmem_limit_bytes=VMEM),
         cost_estimate=COST(2),
         name="forward",
-    )(jnp.asarray(ROW_OF), jnp.asarray(KEY_OF), meta, *in_hbm(pack))
-
-
-def backward_kernel(row_of, key_of, meta, pack, d_in, e_in, o_in, li_in, dq_out, dkv_out, dq, dk, dv, dn, delta, pk, pv):
+    )(jnp.asarray(ROW_OF), jnp.asarray(KEY_OF), meta, *in_hbm(pack, other))
+
+
+def backward_kernel(row_of, key_of, meta, pack, other, d_in, e_in, o_in, li_in, dq_out, keep_out, send_out, dq, dk, dv, dn, delta, pk, pv, kall, vall):
     t = pl.program_id(0)
     rb, kb = row_of[t], key_of[t]
     part = meta[SPLIT]
@@ -196,6 +214,7 @@
     def _():
         pk[...] = prefix_rows(pack, 0)
         pv[...] = prefix_rows(pack, 1)
+        keys_and_values(part, pack, other, kall, vall)
 
     @pl.when(kb == 0)
     def _():
@@ -226,8 +245,8 @@
             dv[to, :] += dot(e, d, 0, 0)
             dk[to, :] += dot(ds, q, 0, 0)
 
-    keys = pack[pl.ds(kb * KC, KC), K0:V0, :].reshape(N, HD)
-    values = pack[pl.ds(kb * KC, KC), V0:P0, :].reshape(N, HD)
+    keys = kall[pl.ds(kb * KC, KC)].reshape(N, HD)
+    values = vall[pl.ds(kb * KC, KC)].reshape(N, HD)
 
     @pl.when(kb < rb)
     def _():
@@ -242,11 +261,21 @@
         for i in range(2):
             tile(i * HALF, HALF, pk[...], pv[...], (0, half + i * PTOT))
         dq_out[...] = dq[...].astype(BF16).reshape(RC, QR, HD)
-        dkv_out[:, 0:TOK, :] = dk[here, :].astype(BF16).reshape(KC, TOK, HD)
-        dkv_out[:, TOK:, :] = (dv[here, :] * (1.0 / SCALE)).astype(BF16).reshape(KC, TOK, HD)
-
-
-def backward(meta, pack, d, e, o, li):
+        grads_k = dk[here, :].astype(BF16).reshape(KC, TOK, HD)
+        grads_v = (dv[here, :] * (1.0 / SCALE)).astype(BF16).reshape(KC, TOK, HD)
+
+        @pl.when(part % 2 == 0)
+        def _():
+            keep_out[...] = grads_k
+            send_out[...] = grads_v
+
+        @pl.when(part % 2 == 1)
+        def _():
+            keep_out[...] = grads_v
+            send_out[...] = grads_k
+
+
+def backward(meta, pack, other, d, e, o, li):
     by_rows = lambda *shape: pl.BlockSpec(shape, lambda t, r, k, m: (r[t],) + (0,) * (len(shape) - 1))
     return pl.pallas_call(
         backward_kernel,
@@ -255,6 +284,7 @@
             grid=(STEPS,),
             in_specs=[
                 pl.BlockSpec((CHUNKS, PACK, HD), lambda t, r, k, m: (0, 0, 0)),
+                pl.BlockSpec((CHUNKS, TOK, HD), lambda t, r, k, m: (0, 0, 0)),
                 by_rows(RC, QR, HD),
                 pl.BlockSpec((1, M, N), lambda t, r, k, m: (t, 0, 0)),
                 by_rows(RC, QR, HD),
@@ -262,7 +292,8 @@
             ],
             out_specs=[
                 by_rows(RC, QR, HD),
-                by_rows(KC, 2 * TOK, HD),
+                by_rows(KC, TOK, HD),
+                by_rows(KC, TOK, HD),
             ],
             scratch_shapes=[
                 pltpu.VMEM((M, HD), F32),
@@ -272,16 +303,19 @@
                 pltpu.VMEM((M, HD), F32),
                 pltpu.VMEM((PTOT, HD), BF16),
                 pltpu.VMEM((PTOT, HD), BF16),
+                pltpu.VMEM((CHUNKS, TOK, HD), BF16),
+                pltpu.VMEM((CHUNKS, TOK, HD), BF16),
             ],
         ),
         out_shape=[
             pltpu.HBM((CHUNKS, QR, HD), BF16),
-            pltpu.HBM((CHUNKS, 2 * TOK, HD), BF16),
+            pltpu.HBM((CHUNKS, TOK, HD), BF16),
+            pltpu.HBM((CHUNKS, TOK, HD), BF16),
         ],
         compiler_params=pltpu.CompilerParams(vmem_limit_bytes=VMEM),
         cost_estimate=COST(4),
         name="backward",
-    )(jnp.asarray(ROW_OF), jnp.asarray(KEY_OF), meta, *in_hbm(pack, d, e, o, li))
+    )(jnp.asarray(ROW_OF), jnp.asarray(KEY_OF), meta, *in_hbm(pack, other, d, e, o, li))
 
 
 GROUPS = CHUNKS // SPLIT
@@ -315,8 +349,7 @@
             prefix = jnp.concatenate([pre_keys[0, :, at].astype(F32), pre_values[0, :, at].astype(F32)], axis=0)
             prefix = prefix.astype(BF16)
             for j in range(SPLIT):
-                out[j, g, K0:V0, :] = keys[0, :, at]
-                out[j, g, V0:P0, :] = values[0, :, at]
+                out[j, g, K0:P0, :] = (values if j % 2 else keys)[0, :, at]
                 out[j, g, P0:PACK, :] = prefix
 
 
@@ -354,11 +387,11 @@
 
 def sum_kernel(parts, keys, values):
     for g in range(AT_ONCE):
-        total = parts[0, g].astype(F32)
-        for j in range(1, SPLIT):
-            total += parts[j, g].astype(F32)
-        keys[0, :, g * HD : (g + 1) * HD] = total[:TOK].astype(BF16)
-        values[0, :, g * HD : (g + 1) * HD] = total[TOK:].astype(BF16)
+        for first, out in ((0, keys), (1, values)):
+            total = parts[first, g].astype(F32)
+            for j in range(first + 2, SPLIT, 2):
+                total += parts[j, g].astype(F32)
+            out[0, :, g * HD : (g + 1) * HD] = total.astype(BF16)
 
 
 def sum_parts(parts):
@@ -366,12 +399,20 @@
     return pl.pallas_call(
         sum_kernel,
         grid=(GROUPS // AT_ONCE,),
-        in_specs=[parts_of(2 * TOK)],
+        in_specs=[parts_of(TOK)],
         out_specs=[cols(TOK, HD), cols(TOK, HD)],
         out_shape=[shape, shape],
         compiler_params=pltpu.CompilerParams(vmem_limit_bytes=VMEM),
         name="sum_parts",
-    )(*in_hbm(parts.reshape(SPLIT, GROUPS, 2 * TOK, HD)))
+    )(*in_hbm(parts.reshape(SPLIT, GROUPS, TOK, HD)))
+
+
+def partner(x):
+    return lax.ppermute(x, "blk", [(i, i ^ 1) for i in range(lax.axis_size("blk"))])
+
+
+def add_partner(keep, send):
+    return (keep.astype(F32) + partner(send).astype(F32)).astype(BF16)
 
 
 def exchange(x):
@@ -388,13 +429,14 @@
     meta = jnp.concatenate([prefix_fill, part[None]])
     pack = exchange(gather(queries, keys, values, pre_keys, pre_values))
     d = exchange(gather(d_out))
-    e, o, li = forward(meta, pack)
+    other = partner(pack[:, K0:P0])
+    e, o, li = forward(meta, pack, other)
     moved_o = shifted(exchange(o), 1)
-    dq, dkv = backward(meta, pack, d, e, o, li)
+    dq, keep, send = backward(meta, pack, other, d, e, o, li)
     moved_dq, moved_o = lax.optimization_barrier((shifted(dq, -1), moved_o))
     query_grad = spread(exchange(moved_dq))
     next_input = spread(moved_o)
-    key_grad, value_grad = (shifted(x, -1) for x in sum_parts(exchange(dkv)))
+    key_grad, value_grad = (shifted(x, -1) for x in sum_parts(exchange(add_partner(keep, send))))
     return (next_input, query_grad, key_grad, value_grad)
 
 

time: 227 us -> 208 us (0.916)
  waiting for transfers between devices: 90.7 us -> 37.7 us
  blocking collectives: 0 us -> 41.8 us
  starting transfers between devices: 41.5 us -> 31.5 us
  other arithmetic: 0.59 us -> 3.16 us
    all_to_all x5 -> x4, waiting for transfers between devices: 45.5 us -> 2.07 us  [exchange(): lax.all_to_all(x, ('blk', 'uly'), split_axis=0, concat_axis=0, tiled=True)]
    all_to_all x0 -> x1, blocking collectives: none -> 41.8 us  [exchange(): lax.all_to_all(x, ('blk', 'uly'), split_axis=0, concat_axis=0, tiled=True)]
    all_to_all x5 -> x4, starting transfers between devices: 37.4 us -> 27.2 us  [exchange(): lax.all_to_all(x, ('blk', 'uly'), split_axis=0, concat_axis=0, tiled=True)]
    ppermute x4, waiting for transfers between devices: 45.2 us -> 35.6 us  [shifted(): lax.ppermute(block, 'section', [((i - distance) % count, i) for i in rang...]
    convert_element_type x0 -> x1, other arithmetic: none -> 2.57 us  [add_partner(): return (keep.astype(F32) + partner(send).astype(F32)).astype(BF16)]
    unnamed x14 -> x16, local copies, waits for them, and re-layouts: 4.87 us -> 5.48 us
  transfers between devices with their start and end apart: 9 -> 10, of which waited for: 6 -> 5; matrix products, arithmetic and copies ran while one was open for 0% -> 2% of each run, Pallas kernels for 36% -> 39%
where the time goes in v4:
time: 208 us; the launch traced here: 207 us
  Pallas kernels  86.9 us (42%)
  blocking collectives  41.8 us (20%)
  waiting for transfers between devices  37.7 us (18%)
  starting transfers between devices  31.5 us (15%)
  local copies, waits for them, and re-layouts  5.6 us (3%)
  other arithmetic  3.16 us (2%)
    all_to_all x1, blocking collectives, exchange(): lax.all_to_all(x, ('blk', 'uly'), split_axis=0, concat_axis=0, tiled=True)  41.8 us
    pallas_call x1, Pallas kernels, forward(): pl.pallas_call(forward_kernel, grid_spec=pltpu.PrefetchScalarGridSpec(num...  37.7 us
    pallas_call x1, Pallas kernels, backward(): pl.pallas_call(backward_kernel, grid_spec=pltpu.PrefetchScalarGridSpec(nu...  37 us
    ppermute x4, waiting for transfers between devices, shifted(): lax.ppermute(block, 'section', [((i - distance) % count, i) for i in rang...  35.6 us
    all_to_all x4, starting transfers between devices, exchange(): lax.all_to_all(x, ('blk', 'uly'), split_axis=0, concat_axis=0, tiled=True)  27.2 us
    pallas_call x2, Pallas kernels, gather(): pl.pallas_call(gather_kernel, grid=(GROUPS // AT_ONCE,), in_specs=[cols(x...  5.77 us
    unnamed x16, local copies, waits for them, and re-layouts  5.48 us
    pallas_call x2, Pallas kernels, spread(): pl.pallas_call(spread_kernel, grid=(GROUPS // AT_ONCE,), in_specs=[parts_...  4.5 us
  transfers between devices with their start and end apart: 10, of which 5 were waited for; matrix products, arithmetic and copies ran while one was open for 2% of the time, Pallas kernels for 39%

profile of v4, /device:TPU:0, one launch (start us, length us, event | category | flops | bytes accessed | tf_op | source)
XLA Modules:
  0.0 207.3 jit_solution(5297071576684837006)
XLA Ops:
  0.6 2.9 %gather.2 = bf16[4,8,304,128]{3,2,1,0:T(8,128)(2,1)} custom-call(bf16[1,128,5120]{2,1,0:T(8,128)(2,1)} %refs_0_.2, bf16[1,128,1024]{2,1,0:T(8,128)(2,1)} %refs_1_.1, bf16[1,128,1024]{2,1,0:T(8,128)(2,1)} %refs_2_.1, bf16[1,8,1024]{2,1,0:T(8,128)(2,1)} %refs_3_.1, bf16[1,8,1024]{2,1,0:T(8,128)(2,1)} %refs_4_.1), custom_call_target="tpu_custom_call" | custom-call | tf_op jit(solution)/shard_map/gather/pallas_call | solution.py:358
  3.5 41.8 %all_to_all.25.pack = bf16[32,304,128]{2,1,0:T(8,128)(2,1)S(1)} all-to-all(bf16[32,304,128]{2,1,0:T(8,128)(2,1)} %bitcast.6), channel_id=1, replica_groups=mesh['section'=4,'blk'=4,'uly'=8] {'blk','uly'}, dimensions={0} | all-to-all | bytes 4980736 | tf_op jit(solution)/shard_map/all_to_all | solution.py:419
  45.2 0.0 copy-start.1
  45.3 0.1 slice.4
  45.4 0.1 collective-permute-start
  45.5 2.9 %gather.3 = bf16[4,8,160,128]{3,2,1,0:T(8,128)(2,1)} custom-call(bf16[1,128,5120]{2,1,0:T(8,128)(2,1)} %refs_0_.3), custom_call_target="tpu_custom_call" | custom-call | tf_op jit(solution)/shard_map/gather/pallas_call | solution.py:358
  48.4 0.0 copy-done.1
  48.4 0.0 copy-start.6
  48.4 5.3 %all-to-all-start.1 = ((bf16[32,160,128]{2,1,0:T(8,128)(2,1)}), bf16[32,160,128]{2,1,0:T(8,128)(2,1)S(1)}, u32[]{:S(2)}, u32[]{:S(2)}) async-start(bf16[32,160,128]{2,1,0:T(8,128)(2,1)} %bitcast.8), calls=%async_computation.1 | async-start | bytes 2621440 | tf_op jit(solution)/shard_map/all_to_all | solution.py:419
  53.7 0.0 copy-done.6
  53.7 0.6 pad_add_fusion.meta
  54.3 0.0 collective-permute-done.other
  54.3 0.0 copy-start.5
  54.3 1.0 copy-done.5
  55.2 37.7 %forward.1 = (bf16[10,1280,1024]{2,1,0:T(8,128)(2,1)}, bf16[32,160,128]{2,1,0:T(8,128)(2,1)}, f32[5120,128]{1,0:T(8,128)}) custom-call(s32[10]{0:T(128)} %constant.9.clone.row_of, s32[10]{0:T(128)} %constant.10.clone.key_of, s32[5]{0:T(128)} %pad_add_fusion.meta, bf16[32,304,128]{2,1,0:T(8,128)(2,1)} %copy-done.1, bf16[32,128,128]{2,1,0:T(8,128)(2,1)} %copy-done.5), custom_call_target="tpu_custom_call" | custom-call | flops 6710886400 | bytes 26214400 | tf_op jit(solution)/shard_map/forward/pallas_call | solution.py:173
  92.9 0.0 all-to-all-done.1.d_in
  92.9 0.0 copy-start.4
  92.9 1.1 copy-done.4
  94.0 7.7 %all-to-all-start.2 = ((bf16[32,160,128]{2,1,0:T(8,128)(2,1)}), bf16[32,160,128]{2,1,0:T(8,128)(2,1)}, u32[]{:S(2)}, u32[]{:S(2)}) async-start(bf16[32,160,128]{2,1,0:T(8,128)(2,1)} %get-tuple-element.15.o_in), calls=%async_computation.2 | async-start | bytes 2621440 | tf_op jit(solution)/shard_map/all_to_all | solution.py:419
  101.7 37.0 %backward.1 = (bf16[32,160,128]{2,1,0:T(8,128)(2,1)}, bf16[32,128,128]{2,1,0:T(8,128)(2,1)}, bf16[32,128,128]{2,1,0:T(8,128)(2,1)}) custom-call(s32[10]{0:T(128)} %constant.9.clone.row_of, s32[10]{0:T(128)} %constant.10.clone.key_of, s32[5]{0:T(128)} %pad_add_fusion.meta, bf16[32,304,128]{2,1,0:T(8,128)(2,1)} %copy-done.1, bf16[32,128,128]{2,1,0:T(8,128)(2,1)} %copy-done.5, ...), custom_call_target="tpu_custom_call" | custom-call | flops 13421772800 | bytes 52428800 | tf_op jit(solution)/shard_map/backward/pallas_call | solution.py:280
  138.6 0.1 collective-permute-start.3
  138.7 2.8 %collective-permute-start.1 = (bf16[32,160,128]{2,1,0:T(8,128)(2,1)}, bf16[32,160,128]{2,1,0:T(8,128)(2,1)S(1)}, u32[]{:S(2)}, u32[]{:S(2)}) collective-permute-start(bf16[32,160,128]{2,1,0:T(8,128)(2,1)} %get-tuple-element.17), channel_id=1, source_target_pairs={{32,0},{64,32},{96,64},{0,96},{33,1},{65,33},{97,65},{1,97},{34,2}... | collective-permute-start | bytes 3932168 | tf_op jit(solution)/shard_map/ppermute | solution.py:424
  141.5 0.0 all-to-all-done.2
  141.5 0.0 collective-permute-start.2
  141.5 0.0 collective-permute-done.3
  141.5 2.6 %add_convert_fusion = bf16[32,128,128]{2,1,0:T(8,128)(2,1)} fusion(bf16[32,128,128]{2,1,0:T(8,128)(2,1)S(1)} %collective-permute-done.3, bf16[32,128,128]{2,1,0:T(8,128)(2,1)} %get-tuple-element.20), kind=kLoop, calls=%fused_computation | loop fusion | flops 2097152 | bytes 3145728 | tf_op jit(solution)/shard_map/convert_element_type | solution.py:415
  144.1 7.2 %all-to-all-start.4 = ((bf16[32,128,128]{2,1,0:T(8,128)(2,1)}), bf16[32,128,128]{2,1,0:T(8,128)(2,1)S(1)}, u32[]{:S(2)}, u32[]{:S(2)}) async-start(bf16[32,128,128]{2,1,0:T(8,128)(2,1)} %add_convert_fusion), calls=%async_computation.4 | async-start | bytes 2097152 | tf_op jit(solution)/shard_map/all_to_all | solution.py:419
  151.3 19.1 %collective-permute-done.1 = bf16[32,160,128]{2,1,0:T(8,128)(2,1)S(1)} collective-permute-done((bf16[32,160,128]{2,1,0:T(8,128)(2,1)}, bf16[32,160,128]{2,1,0:T(8,128)(2,1)S(1)}, u32[]{:S(2)}, u32[]{:S(2)}) %collective-permute-start.1) | collective-permute-done | bytes 1310752 | tf_op jit(solution)/shard_map/ppermute | solution.py:424
  170.5 0.0 copy-start.3
  170.5 3.4 %collective-permute-done.2 = bf16[32,160,128]{2,1,0:T(8,128)(2,1)} collective-permute-done((bf16[32,160,128]{2,1,0:T(8,128)(2,1)}, bf16[32,160,128]{2,1,0:T(8,128)(2,1)}, u32[]{:S(2)}, u32[]{:S(2)}) %collective-permute-start.2) | collective-permute-done | bytes 1310752 | tf_op jit(solution)/shard_map/ppermute | solution.py:424
  173.9 0.0 copy-done.3
  173.9 0.0 all-to-all-done.4
  173.9 0.0 copy-start.2
  173.9 1.0 copy-done.2
  174.9 7.1 %all-to-all-start.3 = ((bf16[32,160,128]{2,1,0:T(8,128)(2,1)}), bf16[32,160,128]{2,1,0:T(8,128)(2,1)S(1)}, u32[]{:S(2)}, u32[]{:S(2)}) async-start(bf16[32,160,128]{2,1,0:T(8,128)(2,1)} %copy-done.3), calls=%async_computation.3 | async-start | bytes 2621440 | tf_op jit(solution)/shard_map/all_to_all | solution.py:419
  182.0 2.0 sum_parts.1
  184.0 1.2 collective-permute-start.4
  185.2 0.0 collective-permute-start.5
  185.2 8.1 %collective-permute-done.4 = bf16[1,128,1024]{2,1,0:T(8,128)(2,1)S(1)} collective-permute-done((bf16[1,128,1024]{2,1,0:T(8,128)(2,1)}, bf16[1,128,1024]{2,1,0:T(8,128)(2,1)S(1)}, u32[]{:S(2)}, u32[]{:S(2)}) %collective-permute-start.4) | collective-permute-done | bytes 262176 | tf_op jit(solution)/shard_map/ppermute | solution.py:424
  193.3 5.0 %collective-permute-done.5 = bf16[1,128,1024]{2,1,0:T(8,128)(2,1)S(1)} collective-permute-done((bf16[1,128,1024]{2,1,0:T(8,128)(2,1)}, bf16[1,128,1024]{2,1,0:T(8,128)(2,1)S(1)}, u32[]{:S(2)}, u32[]{:S(2)}) %collective-permute-start.5) | collective-permute-done | bytes 262176 | tf_op jit(solution)/shard_map/ppermute | solution.py:424
  198.3 2.3 %spread.2 = bf16[1,128,5120]{2,1,0:T(8,128)(2,1)} custom-call(bf16[4,8,160,128]{3,2,1,0:T(8,128)(2,1)} %bitcast.3.packed), custom_call_target="tpu_custom_call" | custom-call | tf_op jit(solution)/shard_map/spread/pallas_call | solution.py:377
  200.5 2.1 all-to-all-done.3
  202.6 0.0 copy-start
  202.6 1.1 copy-done
  203.7 2.3 %spread.3 = bf16[1,128,5120]{2,1,0:T(8,128)(2,1)} custom-call(bf16[4,8,160,128]{3,2,1,0:T(8,128)(2,1)} %bitcast.7), custom_call_target="tpu_custom_call" | custom-call | tf_op jit(solution)/shard_map/spread/pallas_call | solution.py:377
  205.9 0.7 copy.15
  206.6 0.7 copy.16
Async XLA Ops:
  45.2 3.1 %copy-start.1 = (bf16[32,304,128]{2,1,0:T(8,128)(2,1)}, bf16[32,304,128]{2,1,0:T(8,128)(2,1)S(1)}, u32[]{:S(2)}) copy-start(bf16[32,304,128]{2,1,0:T(8,128)(2,1)S(1)} %all_to_all.25.pack) | copy-start | bytes 7471108
  45.4 8.9 %collective-permute-start = (bf16[32,128,128]{2,1,0:T(8,128)(2,1)S(1)}, bf16[32,128,128]{2,1,0:T(8,128)(2,1)S(1)}, u32[]{:S(2)}, u32[]{:S(2)}) collective-permute-start(bf16[32,128,128]{2,1,0:T(8,128)(2,1)S(1)} %slice.4), channel_id=1, source_target_pairs={{0,8},{8,0},{16,24},{24,16},{1,9},{9,1},{17,25},{25,17},{2,10},{10... | collective-permute-start | bytes 3145736 | tf_op jit(solution)/shard_map/ppermute | solution.py:411
  48.4 5.3 %copy-start.6 = (s32[4]{0:T(128)S(1)}, s32[4]{0:T(128)}, u32[]{:S(2)}) copy-start(s32[4]{0:T(128)} %param.15) | copy-start | bytes 52
  48.4 44.6 %all-to-all-start.1 = ((bf16[32,160,128]{2,1,0:T(8,128)(2,1)}), bf16[32,160,128]{2,1,0:T(8,128)(2,1)S(1)}, u32[]{:S(2)}, u32[]{:S(2)}) async-start(bf16[32,160,128]{2,1,0:T(8,128)(2,1)} %bitcast.8), calls=%async_computation.1 | async-start | bytes 2621440 | tf_op jit(solution)/shard_map/all_to_all | solution.py:419
  54.3 1.0 copy-start.5
  92.9 1.1 copy-start.4
  94.0 47.5 %all-to-all-start.2 = ((bf16[32,160,128]{2,1,0:T(8,128)(2,1)}), bf16[32,160,128]{2,1,0:T(8,128)(2,1)}, u32[]{:S(2)}, u32[]{:S(2)}) async-start(bf16[32,160,128]{2,1,0:T(8,128)(2,1)} %get-tuple-element.15.o_in), calls=%async_computation.2 | async-start | bytes 2621440 | tf_op jit(solution)/shard_map/all_to_all | solution.py:419
  138.6 2.9 %collective-permute-start.3 = (bf16[32,128,128]{2,1,0:T(8,128)(2,1)}, bf16[32,128,128]{2,1,0:T(8,128)(2,1)S(1)}, u32[]{:S(2)}, u32[]{:S(2)}) collective-permute-start(bf16[32,128,128]{2,1,0:T(8,128)(2,1)} %get-tuple-element.21), channel_id=1, source_target_pairs={{0,8},{8,0},{16,24},{24,16},{1,9},{9,1},{17,25},{25,17},{2,10},{10... | collective-permute-start | bytes 3145736 | tf_op jit(solution)/shard_map/ppermute | solution.py:411
  138.7 31.7 %collective-permute-start.1 = (bf16[32,160,128]{2,1,0:T(8,128)(2,1)}, bf16[32,160,128]{2,1,0:T(8,128)(2,1)S(1)}, u32[]{:S(2)}, u32[]{:S(2)}) collective-permute-start(bf16[32,160,128]{2,1,0:T(8,128)(2,1)} %get-tuple-element.17), channel_id=1, source_target_pairs={{32,0},{64,32},{96,64},{0,96},{33,1},{65,33},{97,65},{1,97},{34,2}... | collective-permute-start | bytes 3932168 | tf_op jit(solution)/shard_map/ppermute | solution.py:424
  141.5 32.4 %collective-permute-start.2 = (bf16[32,160,128]{2,1,0:T(8,128)(2,1)}, bf16[32,160,128]{2,1,0:T(8,128)(2,1)}, u32[]{:S(2)}, u32[]{:S(2)}) collective-permute-start(bf16[32,160,128]{2,1,0:T(8,128)(2,1)} %all-to-all-done.2), channel_id=1, source_target_pairs={{96,0},{0,32},{32,64},{64,96},{97,1},{1,33},{33,65},{65,97},{98,2}... | collective-permute-start | bytes 3932168 | tf_op jit(solution)/shard_map/ppermute | solution.py:424
  144.1 29.8 %all-to-all-start.4 = ((bf16[32,128,128]{2,1,0:T(8,128)(2,1)}), bf16[32,128,128]{2,1,0:T(8,128)(2,1)S(1)}, u32[]{:S(2)}, u32[]{:S(2)}) async-start(bf16[32,128,128]{2,1,0:T(8,128)(2,1)} %add_convert_fusion), calls=%async_computation.4 | async-start | bytes 2097152 | tf_op jit(solution)/shard_map/all_to_all | solution.py:419
  170.5 3.4 %copy-start.3 = (bf16[32,160,128]{2,1,0:T(8,128)(2,1)}, bf16[32,160,128]{2,1,0:T(8,128)(2,1)S(1)}, u32[]{:S(2)}) copy-start(bf16[32,160,128]{2,1,0:T(8,128)(2,1)S(1)} %collective-permute-done.1) | copy-start | bytes 3932164
  173.9 1.0 copy-start.2
  174.9 27.7 %all-to-all-start.3 = ((bf16[32,160,128]{2,1,0:T(8,128)(2,1)}), bf16[32,160,128]{2,1,0:T(8,128)(2,1)S(1)}, u32[]{:S(2)}, u32[]{:S(2)}) async-start(bf16[32,160,128]{2,1,0:T(8,128)(2,1)} %copy-done.3), calls=%async_computation.3 | async-start | bytes 2621440 | tf_op jit(solution)/shard_map/all_to_all | solution.py:419
  184.0 9.3 %collective-permute-start.4 = (bf16[1,128,1024]{2,1,0:T(8,128)(2,1)}, bf16[1,128,1024]{2,1,0:T(8,128)(2,1)S(1)}, u32[]{:S(2)}, u32[]{:S(2)}) collective-permute-start(bf16[1,128,1024]{2,1,0:T(8,128)(2,1)} %get-tuple-element.22), channel_id=1, source_target_pairs={{32,0},{64,32},{96,64},{0,96},{33,1},{65,33},{97,65},{1,97},{34,2}... | collective-permute-start | bytes 786440 | tf_op jit(solution)/shard_map/ppermute | solution.py:424
  185.2 13.1 %collective-permute-start.5 = (bf16[1,128,1024]{2,1,0:T(8,128)(2,1)}, bf16[1,128,1024]{2,1,0:T(8,128)(2,1)S(1)}, u32[]{:S(2)}, u32[]{:S(2)}) collective-permute-start(bf16[1,128,1024]{2,1,0:T(8,128)(2,1)} %get-tuple-element.23), channel_id=1, source_target_pairs={{32,0},{64,32},{96,64},{0,96},{33,1},{65,33},{97,65},{1,97},{34,2}... | collective-permute-start | bytes 786440 | tf_op jit(solution)/shard_map/ppermute | solution.py:424
  202.6 1.1 copy-start

commit v5 on v4

--- a/solution.py
+++ b/solution.py
@@ -319,7 +319,7 @@
 
 
 GROUPS = CHUNKS // SPLIT
-AT_ONCE = 4
+AT_ONCE = 8
 
 
 def cols(rows, width):

time: 208 us -> 209 us (level)
  transfers between devices with their start and end apart: 10 -> 10, of which waited for: 5 -> 5; matrix products, arithmetic and copies ran while one was open for 2% -> 2% of each run, Pallas kernels for 39% -> 40%
where the time goes in v5:
time: 209 us; the launch traced here: 208 us
  Pallas kernels  88.6 us (42%)
  blocking collectives  41.8 us (20%)
  waiting for transfers between devices  37.2 us (18%)
  starting transfers between devices  31.4 us (15%)
  local copies, waits for them, and re-layouts  5.6 us (3%)
  other arithmetic  3.16 us (2%)
    all_to_all x1, blocking collectives, exchange(): lax.all_to_all(x, ('blk', 'uly'), split_axis=0, concat_axis=0, tiled=True)  41.8 us
    pallas_call x1, Pallas kernels, forward(): pl.pallas_call(forward_kernel, grid_spec=pltpu.PrefetchScalarGridSpec(num...  37.7 us
    pallas_call x1, Pallas kernels, backward(): pl.pallas_call(backward_kernel, grid_spec=pltpu.PrefetchScalarGridSpec(nu...  37 us
    ppermute x4, waiting for transfers between devices, shifted(): lax.ppermute(block, 'section', [((i - distance) % count, i) for i in rang...  35.6 us
    all_to_all x4, starting transfers between devices, exchange(): lax.all_to_all(x, ('blk', 'uly'), split_axis=0, concat_axis=0, tiled=True)  27.2 us
    pallas_call x2, Pallas kernels, gather(): pl.pallas_call(gather_kernel, grid=(GROUPS // AT_ONCE,), in_specs=[cols(x...  6.55 us
    unnamed x16, local copies, waits for them, and re-layouts  5.48 us
    pallas_call x2, Pallas kernels, spread(): pl.pallas_call(spread_kernel, grid=(GROUPS // AT_ONCE,), in_specs=[parts_...  5.19 us
  transfers between devices with their start and end apart: 10, of which 5 were waited for; matrix products, arithmetic and copies ran while one was open for 2% of the time, Pallas kernels for 40%

profile of v5, /device:TPU:0, one launch (start us, length us, event | category | flops | bytes accessed | tf_op | source)
XLA Modules:
  0.0 208.4 jit_solution(15421944081221943318)
XLA Ops:
  0.6 3.3 %gather.2 = bf16[4,8,304,128]{3,2,1,0:T(8,128)(2,1)} custom-call(bf16[1,128,5120]{2,1,0:T(8,128)(2,1)} %refs_0_.2, bf16[1,128,1024]{2,1,0:T(8,128)(2,1)} %refs_1_.1, bf16[1,128,1024]{2,1,0:T(8,128)(2,1)} %refs_2_.1, bf16[1,8,1024]{2,1,0:T(8,128)(2,1)} %refs_3_.1, bf16[1,8,1024]{2,1,0:T(8,128)(2,1)} %refs_4_.1), custom_call_target="tpu_custom_call" | custom-call | tf_op jit(solution)/shard_map/gather/pallas_call | solution.py:358
  3.9 41.8 %all_to_all.25.pack = bf16[32,304,128]{2,1,0:T(8,128)(2,1)S(1)} all-to-all(bf16[32,304,128]{2,1,0:T(8,128)(2,1)} %bitcast.6), channel_id=1, replica_groups=mesh['section'=4,'blk'=4,'uly'=8] {'blk','uly'}, dimensions={0} | all-to-all | bytes 4980736 | tf_op jit(solution)/shard_map/all_to_all | solution.py:419
  45.7 0.0 copy-start.1
  45.7 0.1 slice.4
  45.8 0.1 collective-permute-start
  45.9 3.3 %gather.3 = bf16[4,8,160,128]{3,2,1,0:T(8,128)(2,1)} custom-call(bf16[1,128,5120]{2,1,0:T(8,128)(2,1)} %refs_0_.3), custom_call_target="tpu_custom_call" | custom-call | tf_op jit(solution)/shard_map/gather/pallas_call | solution.py:358
  49.2 0.0 copy-done.1
  49.2 0.0 copy-start.6
  49.2 5.3 %all-to-all-start.1 = ((bf16[32,160,128]{2,1,0:T(8,128)(2,1)}), bf16[32,160,128]{2,1,0:T(8,128)(2,1)S(1)}, u32[]{:S(2)}, u32[]{:S(2)}) async-start(bf16[32,160,128]{2,1,0:T(8,128)(2,1)} %bitcast.8), calls=%async_computation.1 | async-start | bytes 2621440 | tf_op jit(solution)/shard_map/all_to_all | solution.py:419
  54.4 0.0 copy-done.6
  54.5 0.6 pad_add_fusion.meta
  55.0 0.0 collective-permute-done.other
  55.0 0.0 copy-start.5
  55.0 1.0 copy-done.5
  56.0 37.7 %forward.1 = (bf16[10,1280,1024]{2,1,0:T(8,128)(2,1)}, bf16[32,160,128]{2,1,0:T(8,128)(2,1)}, f32[5120,128]{1,0:T(8,128)}) custom-call(s32[10]{0:T(128)} %constant.9.clone.row_of, s32[10]{0:T(128)} %constant.10.clone.key_of, s32[5]{0:T(128)} %pad_add_fusion.meta, bf16[32,304,128]{2,1,0:T(8,128)(2,1)} %copy-done.1, bf16[32,128,128]{2,1,0:T(8,128)(2,1)} %copy-done.5), custom_call_target="tpu_custom_call" | custom-call | flops 6710886400 | bytes 26214400 | tf_op jit(solution)/shard_map/forward/pallas_call | solution.py:173
  93.7 0.0 all-to-all-done.1.d_in
  93.7 0.0 copy-start.4
  93.7 1.1 copy-done.4
  94.8 7.6 %all-to-all-start.2 = ((bf16[32,160,128]{2,1,0:T(8,128)(2,1)}), bf16[32,160,128]{2,1,0:T(8,128)(2,1)}, u32[]{:S(2)}, u32[]{:S(2)}) async-start(bf16[32,160,128]{2,1,0:T(8,128)(2,1)} %get-tuple-element.15.o_in), calls=%async_computation.2 | async-start | bytes 2621440 | tf_op jit(solution)/shard_map/all_to_all | solution.py:419
  102.5 37.0 %backward.1 = (bf16[32,160,128]{2,1,0:T(8,128)(2,1)}, bf16[32,128,128]{2,1,0:T(8,128)(2,1)}, bf16[32,128,128]{2,1,0:T(8,128)(2,1)}) custom-call(s32[10]{0:T(128)} %constant.9.clone.row_of, s32[10]{0:T(128)} %constant.10.clone.key_of, s32[5]{0:T(128)} %pad_add_fusion.meta, bf16[32,304,128]{2,1,0:T(8,128)(2,1)} %copy-done.1, bf16[32,128,128]{2,1,0:T(8,128)(2,1)} %copy-done.5, ...), custom_call_target="tpu_custom_call" | custom-call | flops 13421772800 | bytes 52428800 | tf_op jit(solution)/shard_map/backward/pallas_call | solution.py:280
  139.4 0.1 collective-permute-start.3
  139.5 2.8 %collective-permute-start.1 = (bf16[32,160,128]{2,1,0:T(8,128)(2,1)}, bf16[32,160,128]{2,1,0:T(8,128)(2,1)S(1)}, u32[]{:S(2)}, u32[]{:S(2)}) collective-permute-start(bf16[32,160,128]{2,1,0:T(8,128)(2,1)} %get-tuple-element.17), channel_id=1, source_target_pairs={{32,0},{64,32},{96,64},{0,96},{33,1},{65,33},{97,65},{1,97},{34,2}... | collective-permute-start | bytes 3932168 | tf_op jit(solution)/shard_map/ppermute | solution.py:424
  142.3 0.0 all-to-all-done.2
  142.3 0.0 collective-permute-start.2
  142.3 0.0 collective-permute-done.3
  142.3 2.6 %add_convert_fusion = bf16[32,128,128]{2,1,0:T(8,128)(2,1)} fusion(bf16[32,128,128]{2,1,0:T(8,128)(2,1)S(1)} %collective-permute-done.3, bf16[32,128,128]{2,1,0:T(8,128)(2,1)} %get-tuple-element.20), kind=kLoop, calls=%fused_computation | loop fusion | flops 2097152 | bytes 3145728 | tf_op jit(solution)/shard_map/convert_element_type | solution.py:415
  144.9 7.2 %all-to-all-start.4 = ((bf16[32,128,128]{2,1,0:T(8,128)(2,1)}), bf16[32,128,128]{2,1,0:T(8,128)(2,1)S(1)}, u32[]{:S(2)}, u32[]{:S(2)}) async-start(bf16[32,128,128]{2,1,0:T(8,128)(2,1)} %add_convert_fusion), calls=%async_computation.4 | async-start | bytes 2097152 | tf_op jit(solution)/shard_map/all_to_all | solution.py:419
  152.1 19.1 %collective-permute-done.1 = bf16[32,160,128]{2,1,0:T(8,128)(2,1)S(1)} collective-permute-done((bf16[32,160,128]{2,1,0:T(8,128)(2,1)}, bf16[32,160,128]{2,1,0:T(8,128)(2,1)S(1)}, u32[]{:S(2)}, u32[]{:S(2)}) %collective-permute-start.1) | collective-permute-done | bytes 1310752 | tf_op jit(solution)/shard_map/ppermute | solution.py:424
  171.2 0.0 copy-start.3
  171.2 3.4 %collective-permute-done.2 = bf16[32,160,128]{2,1,0:T(8,128)(2,1)} collective-permute-done((bf16[32,160,128]{2,1,0:T(8,128)(2,1)}, bf16[32,160,128]{2,1,0:T(8,128)(2,1)}, u32[]{:S(2)}, u32[]{:S(2)}) %collective-permute-start.2) | collective-permute-done | bytes 1310752 | tf_op jit(solution)/shard_map/ppermute | solution.py:424
  174.7 0.0 copy-done.3
  174.7 0.0 all-to-all-done.4
  174.7 0.0 copy-start.2
  174.7 1.0 copy-done.2
  175.6 7.1 %all-to-all-start.3 = ((bf16[32,160,128]{2,1,0:T(8,128)(2,1)}), bf16[32,160,128]{2,1,0:T(8,128)(2,1)S(1)}, u32[]{:S(2)}, u32[]{:S(2)}) async-start(bf16[32,160,128]{2,1,0:T(8,128)(2,1)} %copy-done.3), calls=%async_computation.3 | async-start | bytes 2621440 | tf_op jit(solution)/shard_map/all_to_all | solution.py:419
  182.7 2.2 %sum_parts.1 = (bf16[1,128,1024]{2,1,0:T(8,128)(2,1)}, bf16[1,128,1024]{2,1,0:T(8,128)(2,1)}) custom-call(bf16[4,8,128,128]{3,2,1,0:T(8,128)(2,1)} %bitcast.9), custom_call_target="tpu_custom_call" | custom-call | tf_op jit(solution)/shard_map/sum_parts/pallas_call | solution.py:399
  184.9 1.2 collective-permute-start.4
  186.1 0.0 collective-permute-start.5
  186.2 8.1 %collective-permute-done.4 = bf16[1,128,1024]{2,1,0:T(8,128)(2,1)S(1)} collective-permute-done((bf16[1,128,1024]{2,1,0:T(8,128)(2,1)}, bf16[1,128,1024]{2,1,0:T(8,128)(2,1)S(1)}, u32[]{:S(2)}, u32[]{:S(2)}) %collective-permute-start.4) | collective-permute-done | bytes 262176 | tf_op jit(solution)/shard_map/ppermute | solution.py:424
  194.3 5.0 %collective-permute-done.5 = bf16[1,128,1024]{2,1,0:T(8,128)(2,1)S(1)} collective-permute-done((bf16[1,128,1024]{2,1,0:T(8,128)(2,1)}, bf16[1,128,1024]{2,1,0:T(8,128)(2,1)S(1)}, u32[]{:S(2)}, u32[]{:S(2)}) %collective-permute-start.5) | collective-permute-done | bytes 262176 | tf_op jit(solution)/shard_map/ppermute | solution.py:424
  199.2 2.6 %spread.2 = bf16[1,128,5120]{2,1,0:T(8,128)(2,1)} custom-call(bf16[4,8,160,128]{3,2,1,0:T(8,128)(2,1)} %bitcast.3.packed), custom_call_target="tpu_custom_call" | custom-call | tf_op jit(solution)/shard_map/spread/pallas_call | solution.py:377
  201.8 1.5 all-to-all-done.3
  203.4 0.0 copy-start
  203.4 1.1 copy-done
  204.4 2.6 %spread.3 = bf16[1,128,5120]{2,1,0:T(8,128)(2,1)} custom-call(bf16[4,8,160,128]{3,2,1,0:T(8,128)(2,1)} %bitcast.7), custom_call_target="tpu_custom_call" | custom-call | tf_op jit(solution)/shard_map/spread/pallas_call | solution.py:377
  207.0 0.7 copy.15
  207.7 0.7 copy.16
Async XLA Ops:
  45.7 3.5 %copy-start.1 = (bf16[32,304,128]{2,1,0:T(8,128)(2,1)}, bf16[32,304,128]{2,1,0:T(8,128)(2,1)S(1)}, u32[]{:S(2)}) copy-start(bf16[32,304,128]{2,1,0:T(8,128)(2,1)S(1)} %all_to_all.25.pack) | copy-start | bytes 7471108
  45.8 9.2 %collective-permute-start = (bf16[32,128,128]{2,1,0:T(8,128)(2,1)S(1)}, bf16[32,128,128]{2,1,0:T(8,128)(2,1)S(1)}, u32[]{:S(2)}, u32[]{:S(2)}) collective-permute-start(bf16[32,128,128]{2,1,0:T(8,128)(2,1)S(1)} %slice.4), channel_id=1, source_target_pairs={{0,8},{8,0},{16,24},{24,16},{1,9},{9,1},{17,25},{25,17},{2,10},{10... | collective-permute-start | bytes 3145736 | tf_op jit(solution)/shard_map/ppermute | solution.py:411
  49.2 5.3 %copy-start.6 = (s32[4]{0:T(128)S(1)}, s32[4]{0:T(128)}, u32[]{:S(2)}) copy-start(s32[4]{0:T(128)} %param.15) | copy-start | bytes 52
  49.2 44.6 %all-to-all-start.1 = ((bf16[32,160,128]{2,1,0:T(8,128)(2,1)}), bf16[32,160,128]{2,1,0:T(8,128)(2,1)S(1)}, u32[]{:S(2)}, u32[]{:S(2)}) async-start(bf16[32,160,128]{2,1,0:T(8,128)(2,1)} %bitcast.8), calls=%async_computation.1 | async-start | bytes 2621440 | tf_op jit(solution)/shard_map/all_to_all | solution.py:419
  55.0 1.0 copy-start.5
  93.7 1.1 copy-start.4
  94.8 47.5 %all-to-all-start.2 = ((bf16[32,160,128]{2,1,0:T(8,128)(2,1)}), bf16[32,160,128]{2,1,0:T(8,128)(2,1)}, u32[]{:S(2)}, u32[]{:S(2)}) async-start(bf16[32,160,128]{2,1,0:T(8,128)(2,1)} %get-tuple-element.15.o_in), calls=%async_computation.2 | async-start | bytes 2621440 | tf_op jit(solution)/shard_map/all_to_all | solution.py:419
  139.4 2.9 %collective-permute-start.3 = (bf16[32,128,128]{2,1,0:T(8,128)(2,1)}, bf16[32,128,128]{2,1,0:T(8,128)(2,1)S(1)}, u32[]{:S(2)}, u32[]{:S(2)}) collective-permute-start(bf16[32,128,128]{2,1,0:T(8,128)(2,1)} %get-tuple-element.21), channel_id=1, source_target_pairs={{0,8},{8,0},{16,24},{24,16},{1,9},{9,1},{17,25},{25,17},{2,10},{10... | collective-permute-start | bytes 3145736 | tf_op jit(solution)/shard_map/ppermute | solution.py:411
  139.5 31.7 %collective-permute-start.1 = (bf16[32,160,128]{2,1,0:T(8,128)(2,1)}, bf16[32,160,128]{2,1,0:T(8,128)(2,1)S(1)}, u32[]{:S(2)}, u32[]{:S(2)}) collective-permute-start(bf16[32,160,128]{2,1,0:T(8,128)(2,1)} %get-tuple-element.17), channel_id=1, source_target_pairs={{32,0},{64,32},{96,64},{0,96},{33,1},{65,33},{97,65},{1,97},{34,2}... | collective-permute-start | bytes 3932168 | tf_op jit(solution)/shard_map/ppermute | solution.py:424
  142.3 32.4 %collective-permute-start.2 = (bf16[32,160,128]{2,1,0:T(8,128)(2,1)}, bf16[32,160,128]{2,1,0:T(8,128)(2,1)}, u32[]{:S(2)}, u32[]{:S(2)}) collective-permute-start(bf16[32,160,128]{2,1,0:T(8,128)(2,1)} %all-to-all-done.2), channel_id=1, source_target_pairs={{96,0},{0,32},{32,64},{64,96},{97,1},{1,33},{33,65},{65,97},{98,2}... | collective-permute-start | bytes 3932168 | tf_op jit(solution)/shard_map/ppermute | solution.py:424
  144.9 29.8 %all-to-all-start.4 = ((bf16[32,128,128]{2,1,0:T(8,128)(2,1)}), bf16[32,128,128]{2,1,0:T(8,128)(2,1)S(1)}, u32[]{:S(2)}, u32[]{:S(2)}) async-start(bf16[32,128,128]{2,1,0:T(8,128)(2,1)} %add_convert_fusion), calls=%async_computation.4 | async-start | bytes 2097152 | tf_op jit(solution)/shard_map/all_to_all | solution.py:419
  171.2 3.4 %copy-start.3 = (bf16[32,160,128]{2,1,0:T(8,128)(2,1)}, bf16[32,160,128]{2,1,0:T(8,128)(2,1)S(1)}, u32[]{:S(2)}) copy-start(bf16[32,160,128]{2,1,0:T(8,128)(2,1)S(1)} %collective-permute-done.1) | copy-start | bytes 3932164
  174.7 1.0 copy-start.2
  175.6 27.7 %all-to-all-start.3 = ((bf16[32,160,128]{2,1,0:T(8,128)(2,1)}), bf16[32,160,128]{2,1,0:T(8,128)(2,1)S(1)}, u32[]{:S(2)}, u32[]{:S(2)}) async-start(bf16[32,160,128]{2,1,0:T(8,128)(2,1)} %copy-done.3), calls=%async_computation.3 | async-start | bytes 2621440 | tf_op jit(solution)/shard_map/all_to_all | solution.py:419
  184.9 9.3 %collective-permute-start.4 = (bf16[1,128,1024]{2,1,0:T(8,128)(2,1)}, bf16[1,128,1024]{2,1,0:T(8,128)(2,1)S(1)}, u32[]{:S(2)}, u32[]{:S(2)}) collective-permute-start(bf16[1,128,1024]{2,1,0:T(8,128)(2,1)} %get-tuple-element.22), channel_id=1, source_target_pairs={{32,0},{64,32},{96,64},{0,96},{33,1},{65,33},{97,65},{1,97},{34,2}... | collective-permute-start | bytes 786440 | tf_op jit(solution)/shard_map/ppermute | solution.py:424
  186.1 13.1 %collective-permute-start.5 = (bf16[1,128,1024]{2,1,0:T(8,128)(2,1)}, bf16[1,128,1024]{2,1,0:T(8,128)(2,1)S(1)}, u32[]{:S(2)}, u32[]{:S(2)}) collective-permute-start(bf16[1,128,1024]{2,1,0:T(8,128)(2,1)} %get-tuple-element.23), channel_id=1, source_target_pairs={{32,0},{64,32},{96,64},{0,96},{33,1},{65,33},{97,65},{1,97},{34,2}... | collective-permute-start | bytes 786440 | tf_op jit(solution)/shard_map/ppermute | solution.py:424
  203.4 1.1 copy-start
